TPU v7x, 256 devices: a whole 4x4x8 slice. The times are simulated.
256 devices in a mesh: ens: 16 (over x_lo, z), mesh: 16 (over y, x_hi, core).
Axes of the slice: x: 4 (x_hi: 2, x_lo: 2; x = x_hi * 2 + x_lo), y: 4, z: 8, core: 2. Of those that a mesh axis runs over, the one named last changes fastest.
Arguments:
- inputs: bfloat16 [16, 4096, 512], P('ens', 'mesh'), may hold values from -6 to 6
- cotangent: bfloat16 [16, 4096, 512], P('ens', 'mesh'), may hold values from -6 to 6
- noise_level: float32 [16], P('ens'), may hold values from 0.02 to 80
- neighbours: int32 [4096, 32], P('mesh'), may hold values from 0 to 4095, as said below
- live_slots: int32 [4096, 32], P('mesh'), may hold values from 0 to 1
- projections: bfloat16 [2, 4, 512, 512], replicated, may hold values from -4 to 4
- film_weights: float32 [2, 32, 1024], replicated, may hold values from -0.5 to 0.5
Outputs:
- grad_input: bfloat16 [16, 4096, 512], P('ens', 'mesh')
- grad_projections: float32 [2, 4, 512, 512], P(None, None, 'ens', 'mesh')
- grad_film: float32 [2, 32, 1024], P(None, None, 'mesh')
Inputs may be any that keep to these rules, and one draw needn't show every extreme that they name: `neighbours`: slot 0 of node i names i and is live. The live slots of a node name distinct nodes within 128 of it; every node at least 128 from both ends of the numbering has a live slot exactly 128 away. Padded slots name the node itself.
All inputs are finite; a program needn't handle non-finite values.
Results may differ from a plain program's by a relative error of at most 0.028.
Values may be sent and summed in bfloat16 or wider, within the bound.
A program may use at most 64 MiB of HBM per device.

v0:
```python
import math

import jax
import jax.numpy as jnp
from jax import lax
from jax.sharding import PartitionSpec as P

HEADS = 4
NOISE_FREQ = 16
LAYERS = 2


epsilon = 1e-05


def padded(cells, sides, width):
    for axis, dim in sides:
        count = lax.axis_size(axis)
        ends = count - 1
        head = lax.slice_in_dim(cells, 0, width, axis=dim)
        tail = lax.slice_in_dim(cells, cells.shape[dim] - width, cells.shape[dim], axis=dim)
        cells = jnp.concatenate(
            [
                lax.ppermute(tail, axis, [(i, (i + 1) % count) for i in range(ends)]),
                cells,
                lax.ppermute(head, axis, [((i + 1) % count, i) for i in range(ends)]),
            ],
            axis=dim,
        )
    return cells


def from_behind(block, axis, distance):
    devices = range(lax.axis_size(axis))
    route = [(i - distance, i) for i in devices if i - distance in devices]
    return lax.ppermute(block, axis, route)


def noise_features(noise_level):
    frequency = jnp.arange(1, NOISE_FREQ + 1).astype(jnp.float32)
    angles = jnp.log(noise_level)[:, None] * frequency[None, :]
    return jnp.concatenate([jnp.sin(angles), jnp.cos(angles)], axis=1)


def project(left_side, right_side):
    return jnp.dot(left_side, right_side, preferred_element_type=jnp.float32)


def contract_rows(left_side, right_side):
    return lax.dot_general(
        left_side, right_side, (((0,), (0,)), ((), ())), preferred_element_type=jnp.float32
    )


def contract_cols(left_side, right_side):
    return lax.dot_general(
        left_side, right_side, (((1,), (1,)), ((), ())), preferred_element_type=jnp.float32
    )


def normalize(states, film_row, model_width):
    values = states.astype(jnp.float32)
    centre = jnp.mean(values, axis=1, keepdims=True)
    spread = jnp.mean(jnp.square(values - centre), axis=1, keepdims=True)
    inverse = lax.rsqrt(spread + epsilon)
    unit_rows = (values - centre) * inverse
    normed = (unit_rows * (1.0 + film_row[:model_width]) + film_row[model_width:]).astype(
        jnp.bfloat16
    )
    return (unit_rows, inverse, normed)


def dense_attention(query_head, key_head, present, head_size):
    scores = contract_cols(query_head, key_head) / math.sqrt(head_size)
    scores = jnp.where(present, scores, -jnp.inf)
    row_peak = jnp.max(scores, axis=1, keepdims=True)
    weights = jnp.where(present, jnp.exp(scores - row_peak), 0.0)
    return weights / jnp.sum(weights, axis=1, keepdims=True)


def extend_rims(normed, weights, rim_width, model_width):
    joined = jnp.concatenate(
        [
            project(normed, weights[1]).astype(jnp.bfloat16),
            project(normed, weights[2]).astype(jnp.bfloat16),
        ],
        axis=1,
    )
    joined_ext = padded(joined, (("mesh", 0),), rim_width)
    key_ext = joined_ext[:, :model_width]
    value_ext = joined_ext[:, model_width:]
    return (key_ext, value_ext)


def body(inputs, cotangent, noise_level, neighbours, live_slots, projections, film_weights):
    current = inputs[0]
    node_count, model_width = current.shape
    head_size = model_width // HEADS
    rim_width = node_count // 2
    window = node_count + 2 * rim_width
    offset = lax.axis_index("mesh") * node_count - rim_width
    columns = neighbours - offset
    row_ids = jnp.broadcast_to(jnp.arange(node_count, dtype=jnp.int32)[:, None], columns.shape)
    adjacency = (
        jnp.zeros((node_count, window), jnp.float32)
        .at[row_ids, columns]
        .add(live_slots.astype(jnp.float32))
    )
    present = adjacency > 0.5
    embedding = noise_features(noise_level)[0]
    film_rows = [
        jnp.dot(embedding[None, :], film_weights[layer_number], precision=lax.Precision.HIGHEST)[0]
        for layer_number in range(LAYERS)
    ]
    stored = []
    for layer_number in range(LAYERS):
        weights = projections[layer_number]
        unit_rows, inverse, normed = normalize(current, film_rows[layer_number], model_width)
        queries = project(normed, weights[0]).astype(jnp.bfloat16)
        key_ext, value_ext = extend_rims(normed, weights, rim_width, model_width)
        pieces = []
        for head_index in range(HEADS):
            head_cols = slice(head_index * head_size, (head_index + 1) * head_size)
            attention = dense_attention(
                queries[:, head_cols], key_ext[:, head_cols], present, head_size
            )
            pieces.append(project(attention.astype(jnp.bfloat16), value_ext[:, head_cols]))
        attended = jnp.concatenate(pieces, axis=1).astype(jnp.bfloat16)
        stored.append((unit_rows, inverse, normed, queries, key_ext, value_ext, attended))
        current = (current.astype(jnp.float32) + project(attended, weights[3])).astype(jnp.bfloat16)
    upstream = cotangent[0]
    weight_list = [None] * LAYERS
    film_list = [None] * LAYERS
    for layer_number in reversed(range(LAYERS)):
        weights = projections[layer_number]
        film_row = film_rows[layer_number]
        unit_rows, inverse, normed, queries, key_ext, value_ext, attended = stored[layer_number]
        grad_out = contract_rows(attended, upstream)
        grad_attended = contract_cols(upstream, weights[3]).astype(jnp.bfloat16)
        query_parts, key_parts, value_parts = ([], [], [])
        for head_index in range(HEADS):
            head_cols = slice(head_index * head_size, (head_index + 1) * head_size)
            attention = dense_attention(
                queries[:, head_cols], key_ext[:, head_cols], present, head_size
            )
            rounded = attention.astype(jnp.bfloat16)
            grad_head = grad_attended[:, head_cols]
            grad_probs = contract_cols(grad_head, value_ext[:, head_cols])
            grad_scores = (
                attention
                * (grad_probs - jnp.sum(attention * grad_probs, axis=1, keepdims=True))
                / math.sqrt(head_size)
            ).astype(jnp.bfloat16)
            query_parts.append(project(grad_scores, key_ext[:, head_cols]))
            key_parts.append(contract_rows(grad_scores, queries[:, head_cols]))
            value_parts.append(contract_rows(rounded, grad_head))
        grad_queries = jnp.concatenate(query_parts, axis=1).astype(jnp.bfloat16)
        rim_terms = jnp.concatenate(key_parts + value_parts, axis=1)
        from_above = from_behind(rim_terms[:rim_width].astype(jnp.bfloat16), "mesh", -1).astype(
            jnp.float32
        )
        from_below = from_behind(
            rim_terms[rim_width + node_count :].astype(jnp.bfloat16), "mesh", 1
        ).astype(jnp.float32)
        owned_rows = rim_terms[rim_width : rim_width + node_count]
        owned_rows = (
            owned_rows
            + jnp.pad(from_below, ((0, node_count - rim_width), (0, 0)))
            + jnp.pad(from_above, ((node_count - rim_width, 0), (0, 0)))
        )
        grad_keys = owned_rows[:, :model_width].astype(jnp.bfloat16)
        grad_values = owned_rows[:, model_width:].astype(jnp.bfloat16)
        weight_list[layer_number] = jnp.stack(
            [
                contract_rows(normed, grad_queries),
                contract_rows(normed, grad_keys),
                contract_rows(normed, grad_values),
                grad_out,
            ]
        )
        grad_normed = (
            contract_cols(grad_queries, weights[0])
            + contract_cols(grad_keys, weights[1])
            + contract_cols(grad_values, weights[2])
        )
        grad_conditioning = jnp.concatenate(
            [jnp.sum(grad_normed * unit_rows, axis=0), jnp.sum(grad_normed, axis=0)]
        )
        film_list[layer_number] = embedding[:, None] * grad_conditioning[None, :]
        grad_unit = grad_normed * (1.0 + film_row[:model_width])
        centred = (
            grad_unit
            - jnp.mean(grad_unit, axis=1, keepdims=True)
            - unit_rows * jnp.mean(grad_unit * unit_rows, axis=1, keepdims=True)
        )
        upstream = (upstream.astype(jnp.float32) + inverse * centred).astype(jnp.bfloat16)
    weight_grads = jnp.stack(weight_list)
    film_grads = jnp.stack(film_list)
    weight_part, film_part = (
        lax.psum_scatter(
            weight_grads.astype(jnp.bfloat16), "mesh", scatter_dimension=3, tiled=True
        ).astype(jnp.float32),
        lax.psum_scatter(
            film_grads.astype(jnp.bfloat16), "mesh", scatter_dimension=2, tiled=True
        ).astype(jnp.float32),
    )
    weight_out = lax.psum_scatter(
        weight_part.astype(jnp.bfloat16), "ens", scatter_dimension=2, tiled=True
    ).astype(jnp.float32)
    film_out = lax.psum(film_part, "ens")
    return (upstream[None], weight_out, film_out)


def solution(mesh):
    placed = (
        P("ens", "mesh", None),
        P("ens", "mesh", None),
        P("ens"),
        P("mesh", None),
        P("mesh", None),
        P(),
        P(),
    )
    return jax.shard_map(
        body,
        mesh=mesh,
        in_specs=placed,
        out_specs=(P("ens", "mesh", None), P(None, None, "ens", "mesh"), P(None, None, "mesh")),
        check_vma=False,
    )
```

profile of v0, /device:TPU:8, one launch (start us, length us, event | category | flops | bytes accessed | tf_op | source)
XLA Modules:
  0.0 475.2 jit_solution(4812661853184379244)
XLA Ops:
  11.5 1.6 convolution_convert_fusion.14
  13.0 1.4 convolution_convert_fusion.13
  14.5 1.9 collective-permute-start
  16.4 6.0 %collective-permute-start.1 = (bf16[128,1024]{1,0:T(8,128)(2,1)S(1)}, bf16[128,1024]{1,0:T(8,128)(2,1)S(1)}, u32[]{:S(2)}, u32[]{:S(2)}) collective-permute-start(bf16[128,1024]{1,0:T(8,128)(2,1)S(1)} %get-tuple-element.40), channel_id=1, source_target_pairs={{1,0},{2,1},{3,2},{4,3},{5,4},{6,5},{7,6},{8,7},{9,8},{10,9},{11,1... | collective-permute-start | bytes 786440 | tf_op jit(solution)/shard_map/ppermute | solution.py:26
  23.4 56.7 %scatter_custom_fusion = f32[131072]{0:T(1024)S(1)} fusion(s32[8192]{0:T(1024)S(1)} %reshape.328, f32[8192]{0:T(1024)S(1)} %reshape.330, f32[]{:T(128)} %constant.46.clone.1), kind=kCustom, calls=%fused_computation.217 | custom fusion | flops 8192 | bytes 524292
  87.7 1.9 collective-permute-start.2
  89.6 6.2 %collective-permute-start.3 = (bf16[128,1024]{1,0:T(8,128)(2,1)S(1)}, bf16[128,1024]{1,0:T(8,128)(2,1)S(1)}, u32[]{:S(2)}, u32[]{:S(2)}) collective-permute-start(bf16[128,1024]{1,0:T(8,128)(2,1)S(1)} %get-tuple-element.38), channel_id=1, source_target_pairs={{1,0},{2,1},{3,2},{4,3},{5,4},{6,5},{7,6},{8,7},{9,8},{10,9},{11,1... | collective-permute-start | bytes 786440 | tf_op jit(solution)/shard_map/ppermute | solution.py:26
  97.7 1.8 collective-permute-done.3
  107.8 3.4 collective-permute-start.4
  111.2 4.7 collective-permute-start.5
  118.2 1.6 collective-permute-done.5
  127.1 2.9 collective-permute-start.6
  130.0 5.5 %collective-permute-start.7 = (bf16[128,1024]{0,1:T(8,128)(2,1)S(1)}, bf16[128,1024]{0,1:T(8,128)(2,1)S(1)}, u32[]{:S(2)}, u32[]{:S(2)}) collective-permute-start(bf16[128,1024]{0,1:T(8,128)(2,1)S(1)} %get-tuple-element.34), channel_id=1, source_target_pairs={{1,0},{2,1},{3,2},{4,3},{5,4},{6,5},{7,6},{8,7},{9,8},{10,9},{11,1... | collective-permute-start | bytes 786440 | tf_op jit(solution)/shard_map/ppermute | solution.py:36
  137.5 1.6 collective-permute-done.7
  140.5 2.3 pad_maximum_fusion
  142.9 7.9 %copy.17 = bf16[2,4,512,512]{2,1,0,3:T(4,128)(2,1)} copy(bf16[2,4,512,512]{3,2,1,0:T(8,128)(2,1)} %pad_maximum_fusion) | data formatting | bytes 8388608 | tf_op jit(solution)/shard_map/stack | solution.py:197
  153.7 1.6 fusion.36
  158.2 152.6 %all-reduce.7.cloned.1.call-done = bf16[2,4,512,512]{2,1,0,3:T(4,128)(2,1)} async-done(((bf16[2,4,512,512]{2,1,0,3:T(4,128)(2,1)}), bf16[2,4,512,512]{2,1,0,3:T(4,128)(2,1)}) %all-reduce.7.cloned.1.call-update) | async-done | bytes 4194320
  311.8 14.2 %copy.19 = bf16[2,4,512,32]{1,0,3,2:T(2,128)(2,1)} copy(bf16[2,4,512,32]{2,1,0,3:T(4,128)(2,1)S(1)} %constant_dynamic-slice_fusion) | data formatting | bytes 524288
  325.9 17.2 %reshape.338 = bf16[512,256]{1,0:T(8,128)(2,1)} reshape(bf16[512,32,2,4]{3,2,1,0:T(2,128)(2,1)} %bitcast.167) | data formatting | bytes 524288
  344.2 49.2 %reduce-scatter.9.cloned.1.call-done = bf16[64,64]{1,0:T(8,128)(2,1)} async-done(((bf16[1024,64]{1,0:T(8,128)(2,1)}), bf16[64,64]{1,0:T(8,128)(2,1)}) %reduce-scatter.9.cloned.1.call-update) | async-done | bytes 8208
  394.2 63.6 %psum.7 = f32[2,32,64]{2,1,0:T(8,128)} all-reduce(bf16[2,32,64]{2,1,0:T(8,128)(2,1)S(1)} %copy.22), channel_id=1, replica_groups=mesh['ens'=16,'mesh'=16] {'ens'}, use_global_device_ids=true, to_apply=%region_40.41 | all-reduce | flops 4096 | bytes 24576 | tf_op jit(solution)/shard_map/psum | solution.py:210
  457.9 7.4 %reduce-scatter.7.cloned.1.call-done = bf16[32,256]{1,0:T(8,128)(2,1)} async-done(((bf16[512,256]{1,0:T(8,128)(2,1)}), bf16[32,256]{1,0:T(8,128)(2,1)}) %reduce-scatter.7.cloned.1.call-update) | async-done | bytes 16400
  465.2 1.8 reshape.339
  (164 shorter events, 44.0 us)
Async XLA Ops:
  7.2 5.9 %copy-start = (bf16[1,256,512]{2,1,0:T(8,128)(2,1)S(1)}, bf16[1,256,512]{2,1,0:T(8,128)(2,1)}, u32[]{:S(2)}) copy-start(bf16[1,256,512]{2,1,0:T(8,128)(2,1)} %param.7) | copy-start | bytes 786436
  7.2 303.5 %all-reduce.7.cloned.1.call-start = ((), (), s32[]{:S(2)}) async-start(), calls=%async_computation.4 | async-start | bytes 8388608
  11.4 11.1 %copy-start.2 = (f32[2,32,1024]{2,1,0:T(8,128)S(1)}, f32[2,32,1024]{2,1,0:T(8,128)}, u32[]{:S(2)}) copy-start(f32[2,32,1024]{2,1,0:T(8,128)} %param.13) | copy-start | bytes 786436
  11.4 11.3 %copy-start.4 = (s32[256,32]{0,1:T(8,128)S(1)}, s32[256,32]{0,1:T(8,128)}, u32[]{:S(2)}) copy-start(s32[256,32]{0,1:T(8,128)} %param.10) | copy-start | bytes 98308
  11.4 11.4 %copy-start.7 = (s32[2]{0:T(128)S(1)}, s32[2]{0:T(128)}, u32[]{:S(2)}) copy-start(s32[2]{0:T(128)} %constant.74) | copy-start | bytes 28
  11.4 11.4 %copy-start.6 = (s32[2]{0:T(128)S(1)}, s32[2]{0:T(128)}, u32[]{:S(2)}) copy-start(s32[2]{0:T(128)} %constant.71) | copy-start | bytes 28
  11.5 11.5 %copy-start.5 = (s32[256,32]{0,1:T(8,128)S(1)}, s32[256,32]{0,1:T(8,128)}, u32[]{:S(2)}) copy-start(s32[256,32]{0,1:T(8,128)} %param.11) | copy-start | bytes 98308
  14.5 67.3 %collective-permute-start = (bf16[128,1024]{1,0:T(8,128)(2,1)S(1)}, bf16[128,1024]{1,0:T(8,128)(2,1)S(1)}, u32[]{:S(2)}, u32[]{:S(2)}) collective-permute-start(bf16[128,1024]{1,0:T(8,128)(2,1)S(1)} %get-tuple-element.39), channel_id=1, source_target_pairs={{0,1},{1,2},{2,3},{3,4},{4,5},{5,6},{6,7},{7,8},{8,9},{9,10},{10,1... | collective-permute-start | bytes 786440 | tf_op jit(solution)/shard_map/ppermute | solution.py:24
  16.4 65.4 %collective-permute-start.1 = (bf16[128,1024]{1,0:T(8,128)(2,1)S(1)}, bf16[128,1024]{1,0:T(8,128)(2,1)S(1)}, u32[]{:S(2)}, u32[]{:S(2)}) collective-permute-start(bf16[128,1024]{1,0:T(8,128)(2,1)S(1)} %get-tuple-element.40), channel_id=1, source_target_pairs={{1,0},{2,1},{3,2},{4,3},{5,4},{6,5},{7,6},{8,7},{9,8},{10,9},{11,1... | collective-permute-start | bytes 786440 | tf_op jit(solution)/shard_map/ppermute | solution.py:26
  84.0 2.2 copy-start.1
  86.8 9.0 %copy-start.3 = (bf16[1,256,512]{2,1,0:T(8,128)(2,1)S(1)}, bf16[1,256,512]{2,1,0:T(8,128)(2,1)}, u32[]{:S(2)}) copy-start(bf16[1,256,512]{2,1,0:T(8,128)(2,1)} %param.8) | copy-start | bytes 786436
  87.7 10.1 %collective-permute-start.2 = (bf16[128,1024]{1,0:T(8,128)(2,1)S(1)}, bf16[128,1024]{1,0:T(8,128)(2,1)S(1)}, u32[]{:S(2)}, u32[]{:S(2)}) collective-permute-start(bf16[128,1024]{1,0:T(8,128)(2,1)S(1)} %get-tuple-element.37), channel_id=1, source_target_pairs={{0,1},{1,2},{2,3},{3,4},{4,5},{5,6},{6,7},{7,8},{8,9},{9,10},{10,1... | collective-permute-start | bytes 786440 | tf_op jit(solution)/shard_map/ppermute | solution.py:24
  89.6 9.9 %collective-permute-start.3 = (bf16[128,1024]{1,0:T(8,128)(2,1)S(1)}, bf16[128,1024]{1,0:T(8,128)(2,1)S(1)}, u32[]{:S(2)}, u32[]{:S(2)}) collective-permute-start(bf16[128,1024]{1,0:T(8,128)(2,1)S(1)} %get-tuple-element.38), channel_id=1, source_target_pairs={{1,0},{2,1},{3,2},{4,3},{5,4},{6,5},{7,6},{8,7},{9,8},{10,9},{11,1... | collective-permute-start | bytes 786440 | tf_op jit(solution)/shard_map/ppermute | solution.py:26
  107.8 10.4 %collective-permute-start.4 = (bf16[128,1024]{0,1:T(8,128)(2,1)S(1)}, bf16[128,1024]{0,1:T(8,128)(2,1)S(1)}, u32[]{:S(2)}, u32[]{:S(2)}) collective-permute-start(bf16[128,1024]{0,1:T(8,128)(2,1)S(1)} %get-tuple-element.35), channel_id=1, source_target_pairs={{0,1},{1,2},{2,3},{3,4},{4,5},{5,6},{6,7},{7,8},{8,9},{9,10},{10,1... | collective-permute-start | bytes 786440 | tf_op jit(solution)/shard_map/ppermute | solution.py:36
  111.2 8.6 %collective-permute-start.5 = (bf16[128,1024]{0,1:T(8,128)(2,1)S(1)}, bf16[128,1024]{0,1:T(8,128)(2,1)S(1)}, u32[]{:S(2)}, u32[]{:S(2)}) collective-permute-start(bf16[128,1024]{0,1:T(8,128)(2,1)S(1)} %get-tuple-element.36), channel_id=1, source_target_pairs={{1,0},{2,1},{3,2},{4,3},{5,4},{6,5},{7,6},{8,7},{9,8},{10,9},{11,1... | collective-permute-start | bytes 786440 | tf_op jit(solution)/shard_map/ppermute | solution.py:36
  127.1 10.4 %collective-permute-start.6 = (bf16[128,1024]{0,1:T(8,128)(2,1)S(1)}, bf16[128,1024]{0,1:T(8,128)(2,1)S(1)}, u32[]{:S(2)}, u32[]{:S(2)}) collective-permute-start(bf16[128,1024]{0,1:T(8,128)(2,1)S(1)} %get-tuple-element.33), channel_id=1, source_target_pairs={{0,1},{1,2},{2,3},{3,4},{4,5},{5,6},{6,7},{7,8},{8,9},{9,10},{10,1... | collective-permute-start | bytes 786440 | tf_op jit(solution)/shard_map/ppermute | solution.py:36
  130.0 9.1 %collective-permute-start.7 = (bf16[128,1024]{0,1:T(8,128)(2,1)S(1)}, bf16[128,1024]{0,1:T(8,128)(2,1)S(1)}, u32[]{:S(2)}, u32[]{:S(2)}) collective-permute-start(bf16[128,1024]{0,1:T(8,128)(2,1)S(1)} %get-tuple-element.34), channel_id=1, source_target_pairs={{1,0},{2,1},{3,2},{4,3},{5,4},{6,5},{7,6},{8,7},{9,8},{10,9},{11,1... | collective-permute-start | bytes 786440 | tf_op jit(solution)/shard_map/ppermute | solution.py:36
  150.8 242.5 %reduce-scatter.9.cloned.1.call-start = ((), (), s32[]{:S(2)}) async-start(), calls=%async_computation.3 | async-start | bytes 278528
  153.7 3.2 copy-start.8
  156.9 308.4 %reduce-scatter.7.cloned.1.call-start = ((), (), s32[]{:S(2)}) async-start(), calls=%async_computation.2 | async-start | bytes 278528
Sparse Core Ops, SparseCore 0:
  150.9 159.7 all-reduce.6
  314.7 78.6 reduce-scatter.8
  395.8 69.3 reduce-scatter.6
where the time goes:
time: 476 us; the launch traced here: 475 us
  waiting for transfers between devices  218 us (46%)
  other arithmetic  67.9 us (14%)
  blocking collectives  63.6 us (13%)
  local copies, waits for them, and re-layouts  47.9 us (10%)
  starting transfers between devices  32.7 us (7%)
  matrix products  29.3 us (6%)
  between operations  16.1 us (3%)
    unnamed x6, waiting for transfers between devices  209 us
    psum x1, blocking collectives, body(): film_out = lax.psum(film_part, 'ens')  63.6 us
    unnamed x4, other arithmetic  56.9 us
    unnamed x31, local copies, waits for them, and re-layouts  39.6 us
    ppermute x4, starting transfers between devices, from_behind(): return lax.ppermute(block, axis, route)  16.5 us
    ppermute x2, starting transfers between devices, padded(): lax.ppermute(head, axis, [((i + 1) % count, i) for i in range(ends)])  12.3 us
    dot_general x24, matrix products, contract_cols(): lax.dot_general(left_side, right_side, (((1,), (1,)), ((), ())), preferre...  11.8 us
  transfers between devices with their start and end apart: 11, of which 9 were waited for; matrix products, arithmetic and copies ran while one was open for 22% of the time, Pallas kernels for 0%

commit v1 on v0

v1 whole, which is shorter than its diff:
```python
import functools
import math

import jax
import jax.numpy as jnp
from jax import lax
from jax.experimental import pallas as pl
from jax.experimental.pallas import tpu as pltpu
from jax.sharding import PartitionSpec as P

HEADS = 4
NOISE_FREQ = 16
LAYERS = 2
EPSILON = 1e-05
MESH = pl.DeviceIdType.MESH
F32 = jnp.float32
BF16 = jnp.bfloat16
REACH = 128
WIN = 3 * REACH
D = 512
HEAD = D // HEADS
SCALE = 1.0 / math.sqrt(HEAD)


def noise_features(noise_level):
    frequency = jnp.arange(1, NOISE_FREQ + 1).astype(jnp.float32)
    angles = jnp.log(noise_level)[:, None] * frequency[None, :]
    return jnp.concatenate([jnp.sin(angles), jnp.cos(angles)], axis=1)


def nn(a, b):
    return lax.dot_general(a, b, (((1,), (0,)), ((), ())), preferred_element_type=F32)


def nt(a, b):
    return lax.dot_general(a, b, (((1,), (1,)), ((), ())), preferred_element_type=F32)


def kernel(
    ne, nm,
    x_ref, cot_ref, emb_ref, nb_ref, live_ref, w_hbm, fw_ref,
    gin_ref, gw_ref, gf_ref,
    w_v, hx1, hx2, hcot, hup, x2, up1, normed, unit, inv, qe, ke, ve, gae, prob, att,
    bias, bias_t, nl_pad, nl_own, nl_halo, nl_all, stat, stat_own, stat_halo,
    dq, dk, dv, wb, rc, s2, r2, acc, s3, r3, cond, rcond, s2f, r2f, s3f, r3f,
    w_sem, hs_sem, hr_sem, cs_sem, cr_sem, s2_sem, r2_sem, s3_sem, r3_sem,
):
    nq = nm // 2
    cw = D // nm
    rw = D // ne
    e = lax.axis_index("ens")
    m = lax.axis_index("mesh")
    q = m // 2
    core = m % 2
    right = (m + 1) % nm
    left = (m + nm - 1) % nm
    partner = m + 1 - 2 * core
    base = m * (2 * REACH)

    w_copies = {}
    for layer in range(LAYERS):
        for mat in range(4):
            c = pltpu.make_async_copy(w_hbm.at[layer, mat], w_v.at[layer, mat], w_sem.at[layer, mat])
            c.start()
            w_copies[layer, mat] = c

    barrier = pltpu.get_barrier_semaphore()

    def greet(em, mm):
        pl.semaphore_signal(barrier, inc=1, device_id=(em, mm), device_id_type=MESH)

    greet(e, left)
    greet(e, right)
    for k in range(1, nq):
        greet(e, ((q + k) % nq) * 2 + core)
    for k in range(1, ne):
        greet((e + k) % ne, m)
    pl.semaphore_wait(barrier, 2 + (nq - 1) + (ne - 1))

    def rcopy(src, dst, ssem, rsem, em, mm):
        c = pltpu.make_async_remote_copy(
            src_ref=src, dst_ref=dst, send_sem=ssem, recv_sem=rsem, device_id=(em, mm), device_id_type=MESH
        )
        c.start()
        return c

    def halo(kind, low, high, dst):
        a = rcopy(high, dst.at[0], hs_sem.at[kind, 0], hr_sem.at[kind, 0], e, right)
        b = rcopy(low, dst.at[1], hs_sem.at[kind, 1], hr_sem.at[kind, 1], e, left)
        return (a, b)

    def wait_recv(pair):
        for c in pair:
            c.wait_recv()

    sent = []
    LOW, HIGH = pl.ds(0, REACH), pl.ds(REACH, REACH)
    h_x1 = halo(0, x_ref.at[0, LOW], x_ref.at[0, HIGH], hx1)

    nl_pad[...] = jnp.zeros_like(nl_pad)
    nl_pad[:, 0:32] = jnp.where(live_ref[...] > 0, nb_ref[...], -100000).astype(F32)
    for half in range(2):
        nl_own[half] = nl_pad[half * REACH:(half + 1) * REACH, :].T[0:32]
    h_nl = halo(1, nl_own.at[0], nl_own.at[1], nl_halo)
    h_cot = halo(2, cot_ref.at[0, LOW], cot_ref.at[0, HIGH], hcot)
    stat[...] = jnp.zeros_like(stat)
    cond[...] = jnp.zeros_like(cond)
    s3f[...] = jnp.zeros_like(s3f)

    emb = emb_ref[...]
    scales, shifts = [], []
    for layer in range(LAYERS):
        pieces = [
            jnp.sum(emb * fw_ref[layer, :, g * 128:(g + 1) * 128], axis=0, keepdims=True) for g in range(8)
        ]
        row = jnp.concatenate(pieces, axis=1)
        scales.append(1.0 + row[:, :D])
        shifts.append(row[:, D:])

    def normalize(states, layer):
        values = states.astype(F32)
        centre = jnp.mean(values, axis=1, keepdims=True)
        off = values - centre
        spread = jnp.mean(off * off, axis=1, keepdims=True)
        inverse = lax.rsqrt(spread + EPSILON)
        u = off * inverse
        return u, inverse, (u * scales[layer] + shifts[layer]).astype(BF16)

    def project_rows(rows, n, layer):
        w = w_v.at[layer]
        qe[layer, rows] = nn(n, w[0]).astype(BF16)
        ke[layer, rows] = nn(n, w[1]).astype(BF16)
        ve[layer, rows] = nn(n, w[2]).astype(BF16)

    def own_rows(src, layer):
        def step(i, carry):
            rows = pl.ds(pl.multiple_of(i * 64, 64), 64)
            u, inverse, n = normalize(src[rows], layer)
            unit[layer, rows] = u
            inv[layer, rows] = jnp.broadcast_to(inverse, (64, 128))
            normed[layer, rows] = n
            return carry

        lax.fori_loop(0, 4, step, 0)
        project_rows(pl.ds(REACH, 2 * REACH), normed[layer], layer)

    def halo_rows(src, layer):
        for side in range(2):
            _, _, n = normalize(src[side], layer)
            project_rows(pl.ds(side * 3 * REACH, REACH), n, layer)

    def attend(layer):
        for b in range(2):
            rows = pl.ds(REACH + b * REACH, REACH)
            window = pl.ds(b * REACH, WIN)
            for h in range(HEADS):
                cols = slice(h * HEAD, (h + 1) * HEAD)
                s = nt(qe[layer, rows, cols], ke[layer, window, cols]) * SCALE + bias[b]
                peak = jnp.max(s, axis=1, keepdims=True)
                wts = jnp.exp(s - peak)
                total = jnp.sum(wts, axis=1, keepdims=True)
                p = wts * (1.0 / total)
                prob[layer, b * HEADS + h] = p
                stat[layer, b * REACH:(b + 1) * REACH, h:h + 1] = peak + jnp.log(total)
                att[layer, b * REACH:(b + 1) * REACH, cols] = nn(
                    p.astype(BF16), ve[layer, window, cols]
                ).astype(BF16)

    def mask_step(i, carry):
        rows = pl.ds(pl.multiple_of(i * 32, 32), 32)
        first = base - REACH + (i // 4) * REACH
        jid = (lax.broadcasted_iota(jnp.int32, (32, WIN), 1) + first).astype(F32)
        table = nl_pad[rows, 0:32]
        out = jnp.full((32, WIN), -jnp.inf, F32)
        for s in range(32):
            out = jnp.where(table[:, s:s + 1] == jid, 0.0, out)
        bias[i // 4, pl.ds(pl.multiple_of((i % 4) * 32, 32), 32)] = out
        return carry

    for mat in range(3):
        w_copies[0, mat].wait()
    own_rows(x_ref.at[0], 0)
    lax.fori_loop(0, 8, mask_step, 0)
    wait_recv(h_x1)
    halo_rows(hx1, 0)
    attend(0)
    w_copies[0, 3].wait()
    x2[...] = (x_ref[0].astype(F32) + nn(att[0], w_v[0, 3])).astype(BF16)
    h_x2 = halo(3, x2.at[LOW], x2.at[HIGH], hx2)
    for mat in range(4):
        w_copies[1, mat].wait()
    own_rows(x2, 1)

    wait_recv(h_nl)
    nl_all[0] = nl_halo[0]
    nl_all[1] = nl_own[0]
    nl_all[2] = nl_own[1]
    nl_all[3] = nl_halo[1]

    def mask_t_step(i, carry):
        jb = i // 2
        rows = (i % 2) * 64
        jid = (lax.broadcasted_iota(jnp.int32, (64, 128), 0) + (base + jb * REACH + rows)).astype(F32)
        for t in range(3):
            table = nl_all[jb + t]
            out = jnp.full((64, 128), -jnp.inf, F32)
            for s in range(32):
                out = jnp.where(table[s:s + 1, :] == jid, 0.0, out)
            bias_t[jb, pl.ds(pl.multiple_of(rows, 64), 64), t * 128:(t + 1) * 128] = out
        return carry

    lax.fori_loop(0, 4, mask_t_step, 0)

    def grad_attended(up_own, up_halo, layer, which):
        w3 = w_v[layer, 3]
        if which != 1:
            gae[pl.ds(REACH, 2 * REACH)] = nt(up_own, w3).astype(BF16)
        if which != 0:
            for side in range(2):
                gae[pl.ds(side * 3 * REACH, REACH)] = nt(up_halo[side], w3).astype(BF16)

    wait_recv(h_cot)
    grad_attended(cot_ref[0], hcot, 1, 2)
    wait_recv(h_x2)
    halo_rows(hx2, 1)
    attend(1)

    def query_pass(layer):
        for b in range(2):
            rows = pl.ds(REACH + b * REACH, REACH)
            window = pl.ds(b * REACH, WIN)
            for h in range(HEADS):
                cols = slice(h * HEAD, (h + 1) * HEAD)
                gp = nt(gae[rows, cols], ve[layer, window, cols])
                p = prob[layer, b * HEADS + h]
                delta = jnp.sum(p * gp, axis=1, keepdims=True)
                stat[layer, b * REACH:(b + 1) * REACH, HEADS + h:HEADS + h + 1] = delta
                gs = (p * ((gp - delta) * SCALE)).astype(BF16)
                dq[b * REACH:(b + 1) * REACH, cols] = nn(gs, ke[layer, window, cols]).astype(BF16)
        for half in range(2):
            stat_own[layer, half] = stat[layer, half * REACH:(half + 1) * REACH, :].T[0:8]
        return halo(5 + layer, stat_own.at[layer, 0], stat_own.at[layer, 1], stat_halo.at[layer])

    def key_pass(layer):
        for jb in range(2):
            rows = pl.ds(REACH + jb * REACH, REACH)
            window = pl.ds(jb * REACH, WIN)
            if jb == 0:
                parts = [stat_halo[layer, 0], stat_own[layer, 0], stat_own[layer, 1]]
            else:
                parts = [stat_own[layer, 0], stat_own[layer, 1], stat_halo[layer, 1]]
            stats = jnp.concatenate(parts, axis=1)
            for h in range(HEADS):
                cols = slice(h * HEAD, (h + 1) * HEAD)
                queries = qe[layer, window, cols]
                grads = gae[window, cols]
                s = nt(ke[layer, rows, cols], queries) * SCALE + bias_t[jb]
                p = jnp.exp(s - stats[h:h + 1])
                gp = nt(ve[layer, rows, cols], grads)
                gs = (p * ((gp - stats[HEADS + h:HEADS + h + 1]) * SCALE)).astype(BF16)
                dk[jb * REACH:(jb + 1) * REACH, cols] = nn(gs, queries).astype(BF16)
                dv[jb * REACH:(jb + 1) * REACH, cols] = nn(p.astype(BF16), grads).astype(BF16)

    def weight_grad(batch, t, left_side, right_side):
        per = 128 // cw

        def step(cb, carry):
            a = left_side[:, pl.ds(pl.multiple_of(cb * 128, 128), 128)]
            res = nn(a.T, right_side[...]).astype(BF16)
            for u in range(per):
                piece = res[u * cw:(u + 1) * cw]
                if per == 1:
                    wb[batch, cb % 2, t, cb // 2] = piece
                else:
                    wb[batch, u % 2, t, cb * (per // 2) + u // 2] = piece
            return carry

        lax.fori_loop(0, 4, step, 0)

    def start_core(batch):
        return rcopy(wb.at[batch, 1 - core], rc.at[batch], cs_sem.at[batch], cr_sem.at[batch], e, partner)

    def core_sum(batch, copy):
        copy.wait_recv()

        def step(i, carry):
            for t in range(2):
                s2[batch, i, t] = (wb[batch, core, t, i].astype(F32) + rc[batch, t, i].astype(F32)).astype(BF16)
            return carry

        lax.fori_loop(0, nq, step, 0)
        copies = []
        for k in range(1, nq):
            peer = (q + k) % nq
            copies.append(
                rcopy(
                    s2.at[batch, peer], r2.at[batch, k], s2_sem.at[batch, k], r2_sem.at[batch, k],
                    e, peer * 2 + core,
                )
            )
        return copies

    def chip_sum(batch, copies):
        for c in copies:
            c.wait_recv()
        for t in range(2):
            total = s2[batch, q, t].astype(F32)
            for k in range(1, nq):
                total = total + r2[batch, k, t].astype(F32)
            first = ((batch % 2) * 2 + t) * cw
            acc[batch // 2, first:first + cw] = total

    def start_ens(slot):
        whole = acc[slot].T.astype(BF16)
        for i in range(ne):
            s3[slot, i] = whole[i * rw:(i + 1) * rw]
        copies = []
        for k in range(1, ne):
            peer = (e + k) % ne
            copies.append(
                rcopy(s3.at[slot, peer], r3.at[slot, k], s3_sem.at[slot, k], r3_sem.at[slot, k], peer, m)
            )
        return copies

    def ens_sum(slot, copies, layer):
        for c in copies:
            c.wait_recv()
        total = s3[slot, e].astype(F32)
        for k in range(1, ne):
            total = total + r3[slot, k].astype(F32)
        for pos, mat in enumerate((3, 0, 1, 2)):
            gw_ref[layer, mat] = total[:, pos * cw:(pos + 1) * cw]

    def input_pass(layer, up, out):
        w = w_v.at[layer]

        def step(i, carry):
            first, second = carry
            rows = pl.ds(pl.multiple_of(i * 128, 128), 128)
            gn = nt(dq[rows], w[0]) + nt(dk[rows], w[1]) + nt(dv[rows], w[2])
            u = unit[layer, rows]
            gu = gn * u
            first = first + jnp.sum(gu, axis=0, keepdims=True)
            second = second + jnp.sum(gn, axis=0, keepdims=True)
            g = gn * scales[layer]
            mean_g = jnp.mean(g, axis=1, keepdims=True)
            mean_gu = jnp.mean(g * u, axis=1, keepdims=True)
            centred = g - mean_g - u * mean_gu
            out[rows] = (up[rows].astype(F32) + inv[layer, rows][:, 0:1] * centred).astype(BF16)
            return (first, second)

        zero = jnp.zeros((1, D), F32)
        first, second = lax.fori_loop(0, 2, step, (zero, zero))
        row = jnp.concatenate([first, second], axis=1)
        width = 2 * D // nq
        for i in range(nq):
            cond[i, layer:layer + 1] = row[:, i * width:(i + 1) * width]

    st = query_pass(1)
    sent.extend(st)
    weight_grad(0, 0, cot_ref.at[0], att.at[1])
    weight_grad(0, 1, dq, normed.at[1])
    core0 = start_core(0)
    wait_recv(st)
    key_pass(1)
    input_pass(1, cot_ref.at[0], up1)
    h_up = halo(4, up1.at[LOW], up1.at[HIGH], hup)
    weight_grad(1, 0, dk, normed.at[1])
    weight_grad(1, 1, dv, normed.at[1])
    core1 = start_core(1)
    chips0 = core_sum(0, core0)
    grad_attended(up1[...], hup, 0, 0)
    wait_recv(h_up)
    grad_attended(up1, hup, 0, 1)

    st = query_pass(0)
    sent.extend(st)
    chips1 = core_sum(1, core1)
    weight_grad(2, 0, up1, att.at[0])
    weight_grad(2, 1, dq, normed.at[0])
    core2 = start_core(2)
    wait_recv(st)
    key_pass(0)
    chips2 = core_sum(2, core2)
    weight_grad(3, 0, dk, normed.at[0])
    weight_grad(3, 1, dv, normed.at[0])
    core3 = start_core(3)
    input_pass(0, up1, gin_ref.at[0])
    core_f = rcopy(cond, rcond, cs_sem.at[4], cr_sem.at[4], e, partner)
    chips3 = core_sum(3, core3)
    core_f.wait_recv()
    s2f[...] = cond[...] + rcond[...]
    chips_f = []
    for k in range(1, nq):
        peer = (q + k) % nq
        chips_f.append(
            rcopy(s2f.at[peer], r2f.at[k], s2_sem.at[4, k], r2_sem.at[4, k], e, peer * 2 + core)
        )
    chip_sum(0, chips0)
    chip_sum(1, chips1)
    ens_b = start_ens(0)
    for c in chips_f:
        c.wait_recv()
    total = s2f[q]
    for k in range(1, nq):
        total = total + r2f[k]
    s3f[...] = total
    eye = lax.broadcasted_iota(jnp.int32, (32, 128), 0) == lax.broadcasted_iota(jnp.int32, (32, 128), 1)
    s3f[2:3, 0:128] = jnp.sum(jnp.where(eye, emb, 0.0), axis=0, keepdims=True)
    ens_f = []
    for k in range(1, ne):
        ens_f.append(rcopy(s3f, r3f.at[k], s3_sem.at[2, k], r3_sem.at[2, k], (e + k) % ne, m))
    chip_sum(2, chips2)
    chip_sum(3, chips3)
    ens_a = start_ens(1)

    for c in ens_f:
        c.wait_recv()
    films = [None] * LAYERS
    for k in range(ne):
        tile = s3f[...] if k == 0 else r3f[k]
        column = jnp.sum(jnp.where(eye, tile[2:3, 0:128], 0.0), axis=1, keepdims=True)
        for layer in range(LAYERS):
            part = column * tile[layer:layer + 1]
            films[layer] = part if films[layer] is None else films[layer] + part
    half = D // nq
    for layer in range(LAYERS):
        gf_ref[layer] = jnp.where(core == 0, films[layer][:, :half], films[layer][:, half:])
    ens_sum(0, ens_b, 1)
    ens_sum(1, ens_a, 0)

    for pair in (h_x1, h_nl, h_cot, h_x2, h_up):
        sent.extend(pair)
    sent.extend([core0, core1, core2, core3, core_f])
    for group in (chips0, chips1, chips2, chips3, chips_f, ens_a, ens_b, ens_f):
        sent.extend(group)
    for c in sent:
        c.wait_send()


def body(ne, nm, inputs, cotangent, noise_level, neighbours, live_slots, projections, film_weights):
    emb = noise_features(noise_level)[0]
    emb = jnp.broadcast_to(emb[:, None], (2 * NOISE_FREQ, 128))
    nq, cw, rw, fl = nm // 2, D // nm, D // ne, 4 * D // nm
    own = 2 * REACH
    vm = pl.BlockSpec(memory_space=pltpu.VMEM)
    V = pltpu.VMEM
    scratch = [
        V((LAYERS, 4, D, D), BF16),
        V((2, REACH, D), BF16), V((2, REACH, D), BF16), V((2, REACH, D), BF16), V((2, REACH, D), BF16),
        V((own, D), BF16), V((own, D), BF16),
        V((LAYERS, own, D), BF16), V((LAYERS, own, D), F32), V((LAYERS, own, 128), F32),
        V((LAYERS, 2 * own, D), BF16), V((LAYERS, 2 * own, D), BF16), V((LAYERS, 2 * own, D), BF16),
        V((2 * own, D), BF16),
        V((LAYERS, 2 * HEADS, REACH, WIN), F32), V((LAYERS, own, D), BF16),
        V((2, REACH, WIN), F32), V((2, REACH, WIN), F32),
        V((own, 128), F32), V((2, 32, 128), F32), V((2, 32, 128), F32), V((4, 32, 128), F32),
        V((LAYERS, own, 128), F32), V((LAYERS, 2, 8, 128), F32), V((LAYERS, 2, 8, 128), F32),
        V((own, D), BF16), V((own, D), BF16), V((own, D), BF16),
        V((4, 2, 2, nq, cw, D), BF16), V((4, 2, nq, cw, D), BF16),
        V((4, nq, 2, cw, D), BF16), V((4, nq, 2, cw, D), BF16),
        V((2, 4 * cw, D), F32), V((2, ne, rw, 4 * cw), BF16), V((2, ne, rw, 4 * cw), BF16),
        V((nq, 8, fl), F32), V((nq, 8, fl), F32), V((nq, 8, fl), F32), V((nq, 8, fl), F32),
        V((8, fl), F32), V((ne, 8, fl), F32),
        pltpu.SemaphoreType.DMA((LAYERS, 4)),
        pltpu.SemaphoreType.DMA((7, 2)), pltpu.SemaphoreType.DMA((7, 2)),
        pltpu.SemaphoreType.DMA((5,)), pltpu.SemaphoreType.DMA((5,)),
        pltpu.SemaphoreType.DMA((5, nq)), pltpu.SemaphoreType.DMA((5, nq)),
        pltpu.SemaphoreType.DMA((3, ne)), pltpu.SemaphoreType.DMA((3, ne)),
    ]
    return pl.pallas_call(
        functools.partial(kernel, ne, nm),
        out_shape=(
            jax.ShapeDtypeStruct((1, own, D), BF16),
            jax.ShapeDtypeStruct((LAYERS, 4, rw, cw), F32),
            jax.ShapeDtypeStruct((LAYERS, 2 * NOISE_FREQ, fl // 2), F32),
        ),
        in_specs=[vm, vm, vm, vm, vm, pl.BlockSpec(memory_space=pl.ANY), vm],
        out_specs=(vm, vm, vm),
        scratch_shapes=scratch,
        compiler_params=pltpu.CompilerParams(
            collective_id=0, has_side_effects=True, vmem_limit_bytes=56 * 1024 * 1024
        ),
    )(inputs, cotangent, emb, neighbours, live_slots, projections, film_weights)


def solution(mesh):
    placed = (
        P("ens", "mesh", None),
        P("ens", "mesh", None),
        P("ens"),
        P("mesh", None),
        P("mesh", None),
        P(),
        P(),
    )
    return jax.shard_map(
        functools.partial(body, mesh.shape["ens"], mesh.shape["mesh"]),
        mesh=mesh,
        in_specs=placed,
        out_specs=(P("ens", "mesh", None), P(None, None, "ens", "mesh"), P(None, None, "mesh")),
        check_vma=False,
    )
```

time: 476 us -> 89.4 us (0.19)
  waiting for transfers between devices: 218 us -> 0 us
  Pallas kernels: 0 us -> 79.2 us
  other arithmetic: 67.9 us -> 0.12 us
  blocking collectives: 63.6 us -> 0 us
  local copies, waits for them, and re-layouts: 47.9 us -> 8.32 us
  starting transfers between devices: 32.7 us -> 0 us
  matrix products: 29.3 us -> 0 us
  between operations: 16.1 us -> 1.33 us
    unnamed x6 -> x0, waiting for transfers between devices: 209 us -> none
    pallas_call x0 -> x1, Pallas kernels: none -> 79.2 us  [body(): pl.pallas_call(functools.partial(kernel, ne, nm), out_shape=(jax.ShapeDty...]
    psum x1 -> x0, blocking collectives: 63.6 us -> none  [body(): film_out = lax.psum(film_part, 'ens')]
    unnamed x4 -> x0, other arithmetic: 56.9 us -> none
    ppermute x8 -> x0, starting transfers between devices: 32.6 us -> none  [the longest x4 16.5 us: from_behind(): return lax.ppermute(block, axis, route)]
    unnamed x31 -> x5, local copies, waits for them, and re-layouts: 39.6 us -> 7.63 us
    dot_general x73 -> x0, matrix products: 29.3 us -> none  [the longest x24 11.8 us: contract_cols(): lax.dot_general(left_side, right_side, (((1,), (1,)), ((), ())), preferre...]
    ppermute x8 -> x0, waiting for transfers between devices: 8.42 us -> none  [the longest x4 5.38 us: from_behind(): return lax.ppermute(block, axis, route)]
  transfers between devices with their start and end apart: 11 -> 0, of which waited for: 9 -> 0; matrix products, arithmetic and copies ran while one was open for 22% -> 0% of each run, Pallas kernels for 0% -> 0%
where the time goes in v1:
time: 89.4 us; the launch traced here: 89 us
  Pallas kernels  79.2 us (89%)
  local copies, waits for them, and re-layouts  8.32 us (9%)
  between operations  1.33 us (1%)
    pallas_call x1, Pallas kernels, body(): pl.pallas_call(functools.partial(kernel, ne, nm), out_shape=(jax.ShapeDty...  79.2 us
    unnamed x5, local copies, waits for them, and re-layouts  7.63 us

profile of v1, /device:TPU:8, one launch (start us, length us, event | category | flops | bytes accessed | tf_op | source)
XLA Modules:
  0.0 89.0 jit_solution(9949408028679512626)
XLA Ops:
  1.4 0.1 maximum_bitcast_fusion
  1.4 0.7 broadcast_in_dim.10.emb_ref
  2.1 1.5 %copy.10.nb_ref = s32[256,32]{1,0:T(8,128)} copy(s32[256,32]{0,1:T(8,128)} %param.10) | data formatting | bytes 65536 | tf_op args[3]
  3.6 1.5 %copy.11.live_ref = s32[256,32]{1,0:T(8,128)} copy(s32[256,32]{0,1:T(8,128)} %param.11) | data formatting | bytes 65536 | tf_op args[4]
  5.1 79.2 %shard_map.94 = (bf16[1,256,512]{2,1,0:T(8,128)(2,1)}, f32[2,4,32,32]{3,2,1,0:T(8,128)}, f32[2,32,64]{2,1,0:T(8,128)}) custom-call(bf16[1,256,512]{2,1,0:T(8,128)(2,1)} %x_ref.1, bf16[1,256,512]{2,1,0:T(8,128)(2,1)} %cot_ref.1, f32[32,128]{1,0:T(8,128)} %broadcast_in_dim.10.emb_ref, s32[256,32]{1,0:T(8,128)} %copy.10.nb_ref, s32[256,32]{1,0:T(8,128)} %copy.11.live_ref, ...), custom_call_target="tpu_custom_call" | custom-call | tf_op jit(solution)/shard_map/pallas_call | solution.py:471
  84.4 1.7 %copy.16 = bf16[1,256,512]{2,1,0:T(8,128)(2,1)} copy(bf16[1,256,512]{2,1,0:T(8,128)(2,1)} %get-tuple-element.8) | data formatting | bytes 524288
  86.1 1.6 %copy.17 = f32[2,4,32,32]{3,2,1,0:T(8,128)} copy(f32[2,4,32,32]{3,2,1,0:T(8,128)} %get-tuple-element.9) | data formatting | bytes 65536
  87.6 1.4 %copy.18 = f32[2,32,64]{2,1,0:T(8,128)} copy(f32[2,32,64]{2,1,0:T(8,128)} %get-tuple-element.10) | data formatting | bytes 32768
  (1 shorter events, 0.0 us)

commit v2 on v1

--- a/solution.py
+++ b/solution.py
@@ -20,6 +20,7 @@
 D = 512
 HEAD = D // HEADS
 SCALE = 1.0 / math.sqrt(HEAD)
+SCALE2 = SCALE * math.log2(math.e)
 
 
 def noise_features(noise_level):
@@ -41,7 +42,7 @@
     x_ref, cot_ref, emb_ref, nb_ref, live_ref, w_hbm, fw_ref,
     gin_ref, gw_ref, gf_ref,
     w_v, hx1, hx2, hcot, hup, x2, up1, normed, unit, inv, qe, ke, ve, gae, prob, att,
-    bias, bias_t, nl_pad, nl_own, nl_halo, nl_all, stat, stat_own, stat_halo,
+    bias, bias_t, nl_own, nl_halo, stat, stat_own, stat_halo,
     dq, dk, dv, wb, rc, s2, r2, acc, s3, r3, cond, rcond, s2f, r2f, s3f, r3f,
     w_sem, hs_sem, hr_sem, cs_sem, cr_sem, s2_sem, r2_sem, s3_sem, r3_sem,
 ):
@@ -97,12 +98,10 @@
     LOW, HIGH = pl.ds(0, REACH), pl.ds(REACH, REACH)
     h_x1 = halo(0, x_ref.at[0, LOW], x_ref.at[0, HIGH], hx1)
 
-    nl_pad[...] = jnp.zeros_like(nl_pad)
-    nl_pad[:, 0:32] = jnp.where(live_ref[...] > 0, nb_ref[...], -100000).astype(F32)
+    table = jnp.where(live_ref[...] > 0, nb_ref[...], -100000).astype(F32)
     for half in range(2):
-        nl_own[half] = nl_pad[half * REACH:(half + 1) * REACH, :].T[0:32]
+        nl_own[half] = table[:, half * REACH:(half + 1) * REACH]
     h_nl = halo(1, nl_own.at[0], nl_own.at[1], nl_halo)
-    h_cot = halo(2, cot_ref.at[0, LOW], cot_ref.at[0, HIGH], hcot)
     stat[...] = jnp.zeros_like(stat)
     cond[...] = jnp.zeros_like(cond)
     s3f[...] = jnp.zeros_like(s3f)
@@ -155,33 +154,44 @@
             window = pl.ds(b * REACH, WIN)
             for h in range(HEADS):
                 cols = slice(h * HEAD, (h + 1) * HEAD)
-                s = nt(qe[layer, rows, cols], ke[layer, window, cols]) * SCALE + bias[b]
+                s = nt(qe[layer, rows, cols], ke[layer, window, cols]) * SCALE2 + bias[b]
                 peak = jnp.max(s, axis=1, keepdims=True)
-                wts = jnp.exp(s - peak)
+                wts = jnp.exp2(s - peak)
                 total = jnp.sum(wts, axis=1, keepdims=True)
                 p = wts * (1.0 / total)
                 prob[layer, b * HEADS + h] = p
-                stat[layer, b * REACH:(b + 1) * REACH, h:h + 1] = peak + jnp.log(total)
+                stat[layer, b * REACH:(b + 1) * REACH, h:h + 1] = peak + jnp.log2(total)
                 att[layer, b * REACH:(b + 1) * REACH, cols] = nn(
                     p.astype(BF16), ve[layer, window, cols]
                 ).astype(BF16)
 
-    def mask_step(i, carry):
-        rows = pl.ds(pl.multiple_of(i * 32, 32), 32)
-        first = base - REACH + (i // 4) * REACH
-        jid = (lax.broadcasted_iota(jnp.int32, (32, WIN), 1) + first).astype(F32)
-        table = nl_pad[rows, 0:32]
-        out = jnp.full((32, WIN), -jnp.inf, F32)
+    def mask_tile(table, first):
+        jid = (lax.broadcasted_iota(jnp.int32, (REACH, REACH), 0) + first).astype(F32)
+        out = jnp.full((REACH, REACH), -jnp.inf, F32)
         for s in range(32):
-            out = jnp.where(table[:, s:s + 1] == jid, 0.0, out)
-        bias[i // 4, pl.ds(pl.multiple_of((i % 4) * 32, 32), 32)] = out
-        return carry
+            out = jnp.where(table[s:s + 1, :] == jid, 0.0, out)
+        return out
+
+    def own_masks():
+        for b in range(2):
+            for t in range(3):
+                tile = mask_tile(nl_own[b], base + (b + t - 1) * REACH)
+                jb = b + t - 1
+                if 0 <= jb <= 1:
+                    place = b + 1 - jb
+                    bias_t[jb, :, place * REACH:(place + 1) * REACH] = tile
+                bias[b, :, t * REACH:(t + 1) * REACH] = tile.T
+
+    def halo_masks():
+        bias_t[0, :, 0:REACH] = mask_tile(nl_halo[0], base)
+        bias_t[1, :, 2 * REACH:] = mask_tile(nl_halo[1], base + REACH)
 
     for mat in range(3):
         w_copies[0, mat].wait()
     own_rows(x_ref.at[0], 0)
-    lax.fori_loop(0, 8, mask_step, 0)
+    own_masks()
     wait_recv(h_x1)
+    h_cot = halo(2, cot_ref.at[0, LOW], cot_ref.at[0, HIGH], hcot)
     halo_rows(hx1, 0)
     attend(0)
     w_copies[0, 3].wait()
@@ -192,24 +202,7 @@
     own_rows(x2, 1)
 
     wait_recv(h_nl)
-    nl_all[0] = nl_halo[0]
-    nl_all[1] = nl_own[0]
-    nl_all[2] = nl_own[1]
-    nl_all[3] = nl_halo[1]
-
-    def mask_t_step(i, carry):
-        jb = i // 2
-        rows = (i % 2) * 64
-        jid = (lax.broadcasted_iota(jnp.int32, (64, 128), 0) + (base + jb * REACH + rows)).astype(F32)
-        for t in range(3):
-            table = nl_all[jb + t]
-            out = jnp.full((64, 128), -jnp.inf, F32)
-            for s in range(32):
-                out = jnp.where(table[s:s + 1, :] == jid, 0.0, out)
-            bias_t[jb, pl.ds(pl.multiple_of(rows, 64), 64), t * 128:(t + 1) * 128] = out
-        return carry
-
-    lax.fori_loop(0, 4, mask_t_step, 0)
+    halo_masks()
 
     def grad_attended(up_own, up_halo, layer, which):
         w3 = w_v[layer, 3]
@@ -254,61 +247,42 @@
                 cols = slice(h * HEAD, (h + 1) * HEAD)
                 queries = qe[layer, window, cols]
                 grads = gae[window, cols]
-                s = nt(ke[layer, rows, cols], queries) * SCALE + bias_t[jb]
-                p = jnp.exp(s - stats[h:h + 1])
+                s = nt(ke[layer, rows, cols], queries) * SCALE2 + bias_t[jb]
+                p = jnp.exp2(s - stats[h:h + 1])
                 gp = nt(ve[layer, rows, cols], grads)
                 gs = (p * ((gp - stats[HEADS + h:HEADS + h + 1]) * SCALE)).astype(BF16)
                 dk[jb * REACH:(jb + 1) * REACH, cols] = nn(gs, queries).astype(BF16)
                 dv[jb * REACH:(jb + 1) * REACH, cols] = nn(p.astype(BF16), grads).astype(BF16)
 
-    def weight_grad(batch, t, left_side, right_side):
-        per = 128 // cw
-
-        def step(cb, carry):
-            a = left_side[:, pl.ds(pl.multiple_of(cb * 128, 128), 128)]
-            res = nn(a.T, right_side[...]).astype(BF16)
-            for u in range(per):
-                piece = res[u * cw:(u + 1) * cw]
-                if per == 1:
-                    wb[batch, cb % 2, t, cb // 2] = piece
-                else:
-                    wb[batch, u % 2, t, cb * (per // 2) + u // 2] = piece
-            return carry
-
-        lax.fori_loop(0, 4, step, 0)
-
-    def start_core(batch):
+    def weight_grad(batch, left_side, right_side):
+        res = nn(left_side[...].T, right_side[...]).astype(BF16)
+        for i in range(nm):
+            wb[batch, i % 2, i // 2] = res[i * cw:(i + 1) * cw]
         return rcopy(wb.at[batch, 1 - core], rc.at[batch], cs_sem.at[batch], cr_sem.at[batch], e, partner)
 
     def core_sum(batch, copy):
         copy.wait_recv()
-
-        def step(i, carry):
-            for t in range(2):
-                s2[batch, i, t] = (wb[batch, core, t, i].astype(F32) + rc[batch, t, i].astype(F32)).astype(BF16)
-            return carry
-
-        lax.fori_loop(0, nq, step, 0)
         copies = []
-        for k in range(1, nq):
+        for k in range(nq):
             peer = (q + k) % nq
-            copies.append(
-                rcopy(
-                    s2.at[batch, peer], r2.at[batch, k], s2_sem.at[batch, k], r2_sem.at[batch, k],
-                    e, peer * 2 + core,
+            s2[batch, peer] = (wb[batch, core, peer].astype(F32) + rc[batch, peer].astype(F32)).astype(BF16)
+            if k > 0:
+                copies.append(
+                    rcopy(
+                        s2.at[batch, peer], r2.at[batch, k], s2_sem.at[batch, k], r2_sem.at[batch, k],
+                        e, peer * 2 + core,
+                    )
                 )
-            )
         return copies
 
     def chip_sum(batch, copies):
         for c in copies:
             c.wait_recv()
-        for t in range(2):
-            total = s2[batch, q, t].astype(F32)
-            for k in range(1, nq):
-                total = total + r2[batch, k, t].astype(F32)
-            first = ((batch % 2) * 2 + t) * cw
-            acc[batch // 2, first:first + cw] = total
+        total = s2[batch, q].astype(F32)
+        for k in range(1, nq):
+            total = total + r2[batch, k].astype(F32)
+        first = (batch % 4) * cw
+        acc[batch // 4, first:first + cw] = total
 
     def start_ens(slot):
         whole = acc[slot].T.astype(BF16)
@@ -331,74 +305,74 @@
         for pos, mat in enumerate((3, 0, 1, 2)):
             gw_ref[layer, mat] = total[:, pos * cw:(pos + 1) * cw]
 
-    def input_pass(layer, up, out):
+    def input_rows(layer, up, out, i):
         w = w_v.at[layer]
-
-        def step(i, carry):
-            first, second = carry
-            rows = pl.ds(pl.multiple_of(i * 128, 128), 128)
-            gn = nt(dq[rows], w[0]) + nt(dk[rows], w[1]) + nt(dv[rows], w[2])
-            u = unit[layer, rows]
-            gu = gn * u
-            first = first + jnp.sum(gu, axis=0, keepdims=True)
-            second = second + jnp.sum(gn, axis=0, keepdims=True)
-            g = gn * scales[layer]
-            mean_g = jnp.mean(g, axis=1, keepdims=True)
-            mean_gu = jnp.mean(g * u, axis=1, keepdims=True)
-            centred = g - mean_g - u * mean_gu
-            out[rows] = (up[rows].astype(F32) + inv[layer, rows][:, 0:1] * centred).astype(BF16)
-            return (first, second)
-
-        zero = jnp.zeros((1, D), F32)
-        first, second = lax.fori_loop(0, 2, step, (zero, zero))
-        row = jnp.concatenate([first, second], axis=1)
+        rows = pl.ds(i * REACH, REACH)
+        gn = nt(dq[rows], w[0]) + nt(dk[rows], w[1]) + nt(dv[rows], w[2])
+        u = unit[layer, rows]
+        gu = gn * u
+        first = jnp.sum(gu, axis=0, keepdims=True)
+        second = jnp.sum(gn, axis=0, keepdims=True)
+        mean_g = jnp.mean(gn * scales[layer], axis=1, keepdims=True)
+        mean_gu = jnp.mean(gu * scales[layer], axis=1, keepdims=True)
+        centred = gn * scales[layer] - mean_g - u * mean_gu
+        out[rows] = (up[rows].astype(F32) + inv[layer, rows][:, 0:1] * centred).astype(BF16)
+        return jnp.concatenate([first, second], axis=1)
+
+    def put_cond(layer, row):
         width = 2 * D // nq
         for i in range(nq):
             cond[i, layer:layer + 1] = row[:, i * width:(i + 1) * width]
 
+    core_l2o = weight_grad(0, cot_ref.at[0], att.at[1])
     st = query_pass(1)
     sent.extend(st)
-    weight_grad(0, 0, cot_ref.at[0], att.at[1])
-    weight_grad(0, 1, dq, normed.at[1])
-    core0 = start_core(0)
+    core_l2q = weight_grad(1, dq, normed.at[1])
+    chips = {}
+    chips[0] = core_sum(0, core_l2o)
     wait_recv(st)
     key_pass(1)
-    input_pass(1, cot_ref.at[0], up1)
-    h_up = halo(4, up1.at[LOW], up1.at[HIGH], hup)
-    weight_grad(1, 0, dk, normed.at[1])
-    weight_grad(1, 1, dv, normed.at[1])
-    core1 = start_core(1)
-    chips0 = core_sum(0, core0)
+    row = input_rows(1, cot_ref.at[0], up1, 0)
+    up_a = rcopy(up1.at[LOW], hup.at[1], hs_sem.at[4, 1], hr_sem.at[4, 1], e, left)
+    row = row + input_rows(1, cot_ref.at[0], up1, 1)
+    up_b = rcopy(up1.at[HIGH], hup.at[0], hs_sem.at[4, 0], hr_sem.at[4, 0], e, right)
+    put_cond(1, row)
+    core_l2k = weight_grad(2, dk, normed.at[1])
+    core_l2v = weight_grad(3, dv, normed.at[1])
+    chips[1] = core_sum(1, core_l2q)
+    core_l1o = weight_grad(4, up1, att.at[0])
     grad_attended(up1[...], hup, 0, 0)
-    wait_recv(h_up)
-    grad_attended(up1, hup, 0, 1)
 
     st = query_pass(0)
     sent.extend(st)
-    chips1 = core_sum(1, core1)
-    weight_grad(2, 0, up1, att.at[0])
-    weight_grad(2, 1, dq, normed.at[0])
-    core2 = start_core(2)
+    wait_recv((up_a, up_b))
+    grad_attended(up1, hup, 0, 1)
+    core_l1q = weight_grad(5, dq, normed.at[0])
+    chips[2] = core_sum(2, core_l2k)
+    chips[3] = core_sum(3, core_l2v)
     wait_recv(st)
     key_pass(0)
-    chips2 = core_sum(2, core2)
-    weight_grad(3, 0, dk, normed.at[0])
-    weight_grad(3, 1, dv, normed.at[0])
-    core3 = start_core(3)
-    input_pass(0, up1, gin_ref.at[0])
-    core_f = rcopy(cond, rcond, cs_sem.at[4], cr_sem.at[4], e, partner)
-    chips3 = core_sum(3, core3)
+    core_l1k = weight_grad(6, dk, normed.at[0])
+    core_l1v = weight_grad(7, dv, normed.at[0])
+    chips[4] = core_sum(4, core_l1o)
+    chips[5] = core_sum(5, core_l1q)
+    row = input_rows(0, up1, gin_ref.at[0], 0)
+    chips[6] = core_sum(6, core_l1k)
+    row = row + input_rows(0, up1, gin_ref.at[0], 1)
+    put_cond(0, row)
+    core_f = rcopy(cond, rcond, cs_sem.at[8], cr_sem.at[8], e, partner)
+    chips[7] = core_sum(7, core_l1v)
+    for i in range(4):
+        chip_sum(i, chips[i])
+    ens_b = start_ens(0)
     core_f.wait_recv()
     s2f[...] = cond[...] + rcond[...]
     chips_f = []
     for k in range(1, nq):
         peer = (q + k) % nq
         chips_f.append(
-            rcopy(s2f.at[peer], r2f.at[k], s2_sem.at[4, k], r2_sem.at[4, k], e, peer * 2 + core)
+            rcopy(s2f.at[peer], r2f.at[k], s2_sem.at[8, k], r2_sem.at[8, k], e, peer * 2 + core)
         )
-    chip_sum(0, chips0)
-    chip_sum(1, chips1)
-    ens_b = start_ens(0)
     for c in chips_f:
         c.wait_recv()
     total = s2f[q]
@@ -410,8 +384,8 @@
     ens_f = []
     for k in range(1, ne):
         ens_f.append(rcopy(s3f, r3f.at[k], s3_sem.at[2, k], r3_sem.at[2, k], (e + k) % ne, m))
-    chip_sum(2, chips2)
-    chip_sum(3, chips3)
+    for i in range(4, 8):
+        chip_sum(i, chips[i])
     ens_a = start_ens(1)
 
     for c in ens_f:
@@ -429,13 +403,19 @@
     ens_sum(0, ens_b, 1)
     ens_sum(1, ens_a, 0)
 
-    for pair in (h_x1, h_nl, h_cot, h_x2, h_up):
+    for pair in (h_x1, h_nl, h_cot, h_x2, (up_a, up_b)):
         sent.extend(pair)
-    sent.extend([core0, core1, core2, core3, core_f])
-    for group in (chips0, chips1, chips2, chips3, chips_f, ens_a, ens_b, ens_f):
+    sent.extend([core_l2o, core_l2q, core_l2k, core_l2v, core_l1o, core_l1q, core_l1k, core_l1v, core_f])
+    for group in [chips[i] for i in range(8)] + [chips_f, ens_a, ens_b, ens_f]:
         sent.extend(group)
     for c in sent:
         c.wait_send()
+
+
+def hand_over(a_ref, b_ref, c_ref, a_out, b_out, c_out):
+    a_out[...] = a_ref[...]
+    b_out[...] = b_ref[...]
+    c_out[...] = c_ref[...]
 
 
 def body(ne, nm, inputs, cotangent, noise_level, neighbours, live_slots, projections, film_weights):
@@ -454,21 +434,21 @@
         V((2 * own, D), BF16),
         V((LAYERS, 2 * HEADS, REACH, WIN), F32), V((LAYERS, own, D), BF16),
         V((2, REACH, WIN), F32), V((2, REACH, WIN), F32),
-        V((own, 128), F32), V((2, 32, 128), F32), V((2, 32, 128), F32), V((4, 32, 128), F32),
+        V((2, 32, 128), F32), V((2, 32, 128), F32),
         V((LAYERS, own, 128), F32), V((LAYERS, 2, 8, 128), F32), V((LAYERS, 2, 8, 128), F32),
         V((own, D), BF16), V((own, D), BF16), V((own, D), BF16),
-        V((4, 2, 2, nq, cw, D), BF16), V((4, 2, nq, cw, D), BF16),
-        V((4, nq, 2, cw, D), BF16), V((4, nq, 2, cw, D), BF16),
+        V((8, 2, nq, cw, D), BF16), V((8, nq, cw, D), BF16),
+        V((8, nq, cw, D), BF16), V((8, nq, cw, D), BF16),
         V((2, 4 * cw, D), F32), V((2, ne, rw, 4 * cw), BF16), V((2, ne, rw, 4 * cw), BF16),
         V((nq, 8, fl), F32), V((nq, 8, fl), F32), V((nq, 8, fl), F32), V((nq, 8, fl), F32),
         V((8, fl), F32), V((ne, 8, fl), F32),
         pltpu.SemaphoreType.DMA((LAYERS, 4)),
         pltpu.SemaphoreType.DMA((7, 2)), pltpu.SemaphoreType.DMA((7, 2)),
-        pltpu.SemaphoreType.DMA((5,)), pltpu.SemaphoreType.DMA((5,)),
-        pltpu.SemaphoreType.DMA((5, nq)), pltpu.SemaphoreType.DMA((5, nq)),
+        pltpu.SemaphoreType.DMA((9,)), pltpu.SemaphoreType.DMA((9,)),
+        pltpu.SemaphoreType.DMA((9, nq)), pltpu.SemaphoreType.DMA((9, nq)),
         pltpu.SemaphoreType.DMA((3, ne)), pltpu.SemaphoreType.DMA((3, ne)),
     ]
-    return pl.pallas_call(
+    outs = pl.pallas_call(
         functools.partial(kernel, ne, nm),
         out_shape=(
             jax.ShapeDtypeStruct((1, own, D), BF16),
@@ -481,7 +461,13 @@
         compiler_params=pltpu.CompilerParams(
             collective_id=0, has_side_effects=True, vmem_limit_bytes=56 * 1024 * 1024
         ),
-    )(inputs, cotangent, emb, neighbours, live_slots, projections, film_weights)
+    )(inputs, cotangent, emb, neighbours.T, live_slots.T, projections, film_weights)
+    return pl.pallas_call(
+        hand_over,
+        out_shape=tuple(jax.ShapeDtypeStruct(o.shape, o.dtype) for o in outs),
+        in_specs=[vm, vm, vm],
+        out_specs=(vm, vm, vm),
+    )(*outs)
 
 
 def solution(mesh):

time: 89.4 us -> 80 us (0.89)
  local copies, waits for them, and re-layouts: 8.32 us -> 0.68 us
  Pallas kernels: 79.2 us -> 77.1 us
    unnamed x5 -> x0, local copies, waits for them, and re-layouts: 7.63 us -> none
    pallas_call x1, Pallas kernels: 79.2 us -> 75.3 us  [body(): pl.pallas_call(functools.partial(kernel, ne, nm), out_shape=(jax.ShapeDty...]
    pallas_call x0 -> x1, Pallas kernels: none -> 1.78 us  [body(): pl.pallas_call(hand_over, out_shape=tuple((jax.ShapeDtypeStruct(o.shape,...]
where the time goes in v2:
time: 80 us; the launch traced here: 79.2 us
  Pallas kernels  77.1 us (96%)
  between operations  1.33 us (2%)
    pallas_call x1, Pallas kernels, body(): pl.pallas_call(functools.partial(kernel, ne, nm), out_shape=(jax.ShapeDty...  75.3 us
    pallas_call x1, Pallas kernels, body(): pl.pallas_call(hand_over, out_shape=tuple((jax.ShapeDtypeStruct(o.shape,...  1.78 us

profile of v2, /device:TPU:8, one launch (start us, length us, event | category | flops | bytes accessed | tf_op | source)
XLA Modules:
  0.0 79.2 jit_solution(10004316385386866748)
XLA Ops:
  1.4 0.1 maximum_bitcast_fusion
  1.4 0.7 broadcast_in_dim.10.emb_ref
  2.1 75.3 %shard_map.94 = (bf16[1,256,512]{2,1,0:T(8,128)(2,1)}, f32[2,4,32,32]{3,2,1,0:T(8,128)}, f32[2,32,64]{2,1,0:T(8,128)}) custom-call(bf16[1,256,512]{2,1,0:T(8,128)(2,1)} %x_ref.1, bf16[1,256,512]{2,1,0:T(8,128)(2,1)} %cot_ref.1, f32[32,128]{1,0:T(8,128)} %broadcast_in_dim.10.emb_ref, s32[32,256]{1,0:T(8,128)} %bitcast.5, s32[32,256]{1,0:T(8,128)} %bitcast.6, ...), custom_call_target="tpu_custom_call" | custom-call | tf_op jit(solution)/shard_map/pallas_call | solution.py:451
  77.4 1.8 %shard_map.95 = (bf16[1,256,512]{2,1,0:T(8,128)(2,1)}, f32[2,4,32,32]{3,2,1,0:T(8,128)}, f32[2,32,64]{2,1,0:T(8,128)}) custom-call(bf16[1,256,512]{2,1,0:T(8,128)(2,1)} %get-tuple-element.6.a_ref, f32[2,4,32,32]{3,2,1,0:T(8,128)} %get-tuple-element.7.b_ref, f32[2,32,64]{2,1,0:T(8,128)} %get-tuple-element.8.c_ref), custom_call_target="tpu_custom_call" | custom-call | tf_op jit(solution)/shard_map/pallas_call | solution.py:465
  (1 shorter events, 0.0 us)

commit v3 on v2

--- a/solution.py
+++ b/solution.py
@@ -43,20 +43,33 @@
     gin_ref, gw_ref, gf_ref,
     w_v, hx1, hx2, hcot, hup, x2, up1, normed, unit, inv, qe, ke, ve, gae, prob, att,
     bias, bias_t, nl_own, nl_halo, stat, stat_own, stat_halo,
-    dq, dk, dv, wb, rc, s2, r2, acc, s3, r3, cond, rcond, s2f, r2f, s3f, r3f,
-    w_sem, hs_sem, hr_sem, cs_sem, cr_sem, s2_sem, r2_sem, s3_sem, r3_sem,
+    dq, dk, dv, wb, rc, s2, r2, t2, rt, acc, s3, r3, cond, rcond, s2f, ryf, sxf, rxf, s3f, r3f,
+    w_sem, hs_sem, hr_sem, cs_sem, cr_sem, s2_sem, r2_sem, t2_sem, rt_sem, s3_sem, r3_sem,
 ):
     nq = nm // 2
     cw = D // nm
     rw = D // ne
     e = lax.axis_index("ens")
     m = lax.axis_index("mesh")
-    q = m // 2
+    ny, nz = nm // 4, ne // 2
     core = m % 2
+    y = m // 4
+    z = e % nz
+    x = (m // 2) % 2 * 2 + e // nz
     right = (m + 1) % nm
     left = (m + nm - 1) % nm
     partner = m + 1 - 2 * core
     base = m * (2 * REACH)
+
+    def at_y(k):
+        return e, (y + k) % ny * 4 + m % 4
+
+    def at_x(k):
+        there = (x + k) % 4
+        return there % 2 * nz + z, y * 4 + there // 2 * 2 + core
+
+    def at_z(k):
+        return e // nz * nz + (z + k) % nz, m
 
     w_copies = {}
     for layer in range(LAYERS):
@@ -72,11 +85,13 @@
 
     greet(e, left)
     greet(e, right)
-    for k in range(1, nq):
-        greet(e, ((q + k) % nq) * 2 + core)
-    for k in range(1, ne):
-        greet((e + k) % ne, m)
-    pl.semaphore_wait(barrier, 2 + (nq - 1) + (ne - 1))
+    for k in range(1, ny):
+        greet(*at_y(k))
+    for k in range(1, 4):
+        greet(*at_x(k))
+    for k in range(1, nz):
+        greet(*at_z(k))
+    pl.semaphore_wait(barrier, 2 + (ny - 1) + 3 + (nz - 1))
 
     def rcopy(src, dst, ssem, rsem, em, mm):
         c = pltpu.make_async_remote_copy(
@@ -104,7 +119,6 @@
     h_nl = halo(1, nl_own.at[0], nl_own.at[1], nl_halo)
     stat[...] = jnp.zeros_like(stat)
     cond[...] = jnp.zeros_like(cond)
-    s3f[...] = jnp.zeros_like(s3f)
 
     emb = emb_ref[...]
     scales, shifts = [], []
@@ -254,53 +268,73 @@
                 dk[jb * REACH:(jb + 1) * REACH, cols] = nn(gs, queries).astype(BF16)
                 dv[jb * REACH:(jb + 1) * REACH, cols] = nn(p.astype(BF16), grads).astype(BF16)
 
+    def order(batch):
+        return ((ny, y, at_y), (4, x, at_x)) if batch % 2 == 0 else ((4, x, at_x), (ny, y, at_y))
+
     def weight_grad(batch, left_side, right_side):
         res = nn(left_side[...].T, right_side[...]).astype(BF16)
         for i in range(nm):
-            wb[batch, i % 2, i // 2] = res[i * cw:(i + 1) * cw]
+            for xl in range(2):
+                py, px = i // 4, i // 2 % 2 * 2 + xl
+                place = py * 4 + px if batch % 2 == 0 else px * ny + py
+                wb[batch, i % 2, place] = res[i * cw:(i + 1) * cw, xl * 256:(xl + 1) * 256]
         return rcopy(wb.at[batch, 1 - core], rc.at[batch], cs_sem.at[batch], cr_sem.at[batch], e, partner)
 
     def core_sum(batch, copy):
         copy.wait_recv()
+        (n1, c1, at1), (n2, _, _) = order(batch)
         copies = []
-        for k in range(nq):
-            peer = (q + k) % nq
-            s2[batch, peer] = (wb[batch, core, peer].astype(F32) + rc[batch, peer].astype(F32)).astype(BF16)
+        for k in list(range(1, n1)) + [0]:
+            block = pl.ds((c1 + k) % n1 * n2, n2)
+            s2[batch, block] = (wb[batch, core, block].astype(F32) + rc[batch, block].astype(F32)).astype(BF16)
             if k > 0:
                 copies.append(
                     rcopy(
-                        s2.at[batch, peer], r2.at[batch, k], s2_sem.at[batch, k], r2_sem.at[batch, k],
-                        e, peer * 2 + core,
+                        s2.at[batch, block], r2.at[batch, k, pl.ds(0, n2)],
+                        s2_sem.at[batch, k], r2_sem.at[batch, k], *at1(k),
                     )
                 )
         return copies
 
-    def chip_sum(batch, copies):
+    def first_sum(batch, copies):
+        (n1, c1, _), (n2, c2, at2) = order(batch)
         for c in copies:
             c.wait_recv()
-        total = s2[batch, q].astype(F32)
-        for k in range(1, nq):
-            total = total + r2[batch, k].astype(F32)
+        total = s2[batch, pl.ds(c1 * n2, n2)].astype(F32)
+        for k in range(1, n1):
+            total = total + r2[batch, k, 0:n2].astype(F32)
+        t2[batch, 0:n2] = total.astype(BF16)
+        return [
+            rcopy(
+                t2.at[batch, (c2 + k) % n2], rt.at[batch, k], t2_sem.at[batch, k], rt_sem.at[batch, k], *at2(k)
+            )
+            for k in range(1, n2)
+        ]
+
+    def second_sum(batch, copies):
+        _, (n2, c2, _) = order(batch)
+        for c in copies:
+            c.wait_recv()
+        total = t2[batch, c2].astype(F32)
+        for k in range(1, n2):
+            total = total + rt[batch, k].astype(F32)
         first = (batch % 4) * cw
         acc[batch // 4, first:first + cw] = total
 
-    def start_ens(slot):
+    def start_z(slot):
         whole = acc[slot].T.astype(BF16)
-        for i in range(ne):
+        for i in range(nz):
             s3[slot, i] = whole[i * rw:(i + 1) * rw]
-        copies = []
-        for k in range(1, ne):
-            peer = (e + k) % ne
-            copies.append(
-                rcopy(s3.at[slot, peer], r3.at[slot, k], s3_sem.at[slot, k], r3_sem.at[slot, k], peer, m)
-            )
-        return copies
-
-    def ens_sum(slot, copies, layer):
+        return [
+            rcopy(s3.at[slot, (z + k) % nz], r3.at[slot, k], s3_sem.at[slot, k], r3_sem.at[slot, k], *at_z(k))
+            for k in range(1, nz)
+        ]
+
+    def z_sum(slot, copies, layer):
         for c in copies:
             c.wait_recv()
-        total = s3[slot, e].astype(F32)
-        for k in range(1, ne):
+        total = s3[slot, z].astype(F32)
+        for k in range(1, nz):
             total = total + r3[slot, k].astype(F32)
         for pos, mat in enumerate((3, 0, 1, 2)):
             gw_ref[layer, mat] = total[:, pos * cw:(pos + 1) * cw]
@@ -324,12 +358,12 @@
         for i in range(nq):
             cond[i, layer:layer + 1] = row[:, i * width:(i + 1) * width]
 
-    core_l2o = weight_grad(0, cot_ref.at[0], att.at[1])
+    core_of, ring_of, turn_of = {}, {}, {}
+    core_of[0] = weight_grad(0, cot_ref.at[0], att.at[1])
     st = query_pass(1)
     sent.extend(st)
-    core_l2q = weight_grad(1, dq, normed.at[1])
-    chips = {}
-    chips[0] = core_sum(0, core_l2o)
+    core_of[1] = weight_grad(1, dq, normed.at[1])
+    ring_of[0] = core_sum(0, core_of[0])
     wait_recv(st)
     key_pass(1)
     row = input_rows(1, cot_ref.at[0], up1, 0)
@@ -337,76 +371,91 @@
     row = row + input_rows(1, cot_ref.at[0], up1, 1)
     up_b = rcopy(up1.at[HIGH], hup.at[0], hs_sem.at[4, 0], hr_sem.at[4, 0], e, right)
     put_cond(1, row)
-    core_l2k = weight_grad(2, dk, normed.at[1])
-    core_l2v = weight_grad(3, dv, normed.at[1])
-    chips[1] = core_sum(1, core_l2q)
-    core_l1o = weight_grad(4, up1, att.at[0])
+    core_of[2] = weight_grad(2, dk, normed.at[1])
+    core_of[3] = weight_grad(3, dv, normed.at[1])
+    ring_of[1] = core_sum(1, core_of[1])
+    core_of[4] = weight_grad(4, up1, att.at[0])
     grad_attended(up1[...], hup, 0, 0)
 
     st = query_pass(0)
     sent.extend(st)
+    core_of[5] = weight_grad(5, dq, normed.at[0])
+    ring_of[2] = core_sum(2, core_of[2])
+    ring_of[3] = core_sum(3, core_of[3])
+    turn_of[0] = first_sum(0, ring_of[0])
+    ring_of[4] = core_sum(4, core_of[4])
     wait_recv((up_a, up_b))
     grad_attended(up1, hup, 0, 1)
-    core_l1q = weight_grad(5, dq, normed.at[0])
-    chips[2] = core_sum(2, core_l2k)
-    chips[3] = core_sum(3, core_l2v)
     wait_recv(st)
     key_pass(0)
-    core_l1k = weight_grad(6, dk, normed.at[0])
-    core_l1v = weight_grad(7, dv, normed.at[0])
-    chips[4] = core_sum(4, core_l1o)
-    chips[5] = core_sum(5, core_l1q)
+    core_of[6] = weight_grad(6, dk, normed.at[0])
+    core_of[7] = weight_grad(7, dv, normed.at[0])
+    ring_of[5] = core_sum(5, core_of[5])
+    turn_of[1] = first_sum(1, ring_of[1])
     row = input_rows(0, up1, gin_ref.at[0], 0)
-    chips[6] = core_sum(6, core_l1k)
+    ring_of[6] = core_sum(6, core_of[6])
+    ring_of[7] = core_sum(7, core_of[7])
     row = row + input_rows(0, up1, gin_ref.at[0], 1)
     put_cond(0, row)
     core_f = rcopy(cond, rcond, cs_sem.at[8], cr_sem.at[8], e, partner)
-    chips[7] = core_sum(7, core_l1v)
-    for i in range(4):
-        chip_sum(i, chips[i])
-    ens_b = start_ens(0)
+    for i in (2, 3, 4, 5):
+        turn_of[i] = first_sum(i, ring_of[i])
+
     core_f.wait_recv()
     s2f[...] = cond[...] + rcond[...]
-    chips_f = []
-    for k in range(1, nq):
-        peer = (q + k) % nq
-        chips_f.append(
-            rcopy(s2f.at[peer], r2f.at[k], s2_sem.at[8, k], r2_sem.at[8, k], e, peer * 2 + core)
-        )
-    for c in chips_f:
+    y_f = [
+        rcopy(s2f.at[pl.ds((y + k) % ny * 2, 2)], ryf.at[k], s3_sem.at[2, k], r3_sem.at[2, k], *at_y(k))
+        for k in range(1, ny)
+    ]
+    for i in range(4):
+        second_sum(i, turn_of[i])
+    z_b = start_z(0)
+    for c in y_f:
         c.wait_recv()
-    total = s2f[q]
-    for k in range(1, nq):
-        total = total + r2f[k]
-    s3f[...] = total
+    total = s2f[pl.ds(y * 2, 2)]
+    for k in range(1, ny):
+        total = total + ryf[k]
+    sxf[...] = total
     eye = lax.broadcasted_iota(jnp.int32, (32, 128), 0) == lax.broadcasted_iota(jnp.int32, (32, 128), 1)
-    s3f[2:3, 0:128] = jnp.sum(jnp.where(eye, emb, 0.0), axis=0, keepdims=True)
-    ens_f = []
-    for k in range(1, ne):
-        ens_f.append(rcopy(s3f, r3f.at[k], s3_sem.at[2, k], r3_sem.at[2, k], (e + k) % ne, m))
+    emb_row = jnp.sum(jnp.where(eye, emb, 0.0), axis=0, keepdims=True)
+    for half in range(2):
+        sxf[half, 2:3, 0:128] = emb_row
+    x_f = [
+        rcopy(sxf.at[(x + k) % 4 // 2], rxf.at[k], s3_sem.at[3, k], r3_sem.at[3, k], *at_x(k)) for k in range(1, 4)
+    ]
+    for i in (6, 7):
+        turn_of[i] = first_sum(i, ring_of[i])
+    for c in x_f:
+        c.wait_recv()
+    own = sxf[x // 2]
+    first_row = lax.broadcasted_iota(jnp.int32, own.shape, 0) < 2
+    s3f[0] = own + jnp.where(first_row, rxf[2], 0.0)
+    s3f[1] = rxf[1] + jnp.where(first_row, rxf[3], 0.0)
+    z_f = [rcopy(s3f, r3f.at[k], s3_sem.at[4, k], r3_sem.at[4, k], *at_z(k)) for k in range(1, nz)]
     for i in range(4, 8):
-        chip_sum(i, chips[i])
-    ens_a = start_ens(1)
-
-    for c in ens_f:
+        second_sum(i, turn_of[i])
+    z_a = start_z(1)
+
+    for c in z_f:
         c.wait_recv()
     films = [None] * LAYERS
-    for k in range(ne):
-        tile = s3f[...] if k == 0 else r3f[k]
-        column = jnp.sum(jnp.where(eye, tile[2:3, 0:128], 0.0), axis=1, keepdims=True)
-        for layer in range(LAYERS):
-            part = column * tile[layer:layer + 1]
-            films[layer] = part if films[layer] is None else films[layer] + part
-    half = D // nq
+    for k in range(nz):
+        for member in range(2):
+            tile = s3f[member] if k == 0 else r3f[k, member]
+            column = jnp.sum(jnp.where(eye, tile[2:3, 0:128], 0.0), axis=1, keepdims=True)
+            for layer in range(LAYERS):
+                part = column * tile[layer:layer + 1]
+                films[layer] = part if films[layer] is None else films[layer] + part
+    half = 2 * D // nm
     for layer in range(LAYERS):
         gf_ref[layer] = jnp.where(core == 0, films[layer][:, :half], films[layer][:, half:])
-    ens_sum(0, ens_b, 1)
-    ens_sum(1, ens_a, 0)
+    z_sum(0, z_b, 1)
+    z_sum(1, z_a, 0)
 
     for pair in (h_x1, h_nl, h_cot, h_x2, (up_a, up_b)):
         sent.extend(pair)
-    sent.extend([core_l2o, core_l2q, core_l2k, core_l2v, core_l1o, core_l1q, core_l1k, core_l1v, core_f])
-    for group in [chips[i] for i in range(8)] + [chips_f, ens_a, ens_b, ens_f]:
+    sent.extend([core_of[i] for i in range(8)] + [core_f])
+    for group in [g[i] for g in (ring_of, turn_of) for i in range(8)] + [y_f, x_f, z_f, z_a, z_b]:
         sent.extend(group)
     for c in sent:
         c.wait_send()
@@ -422,6 +471,7 @@
     emb = noise_features(noise_level)[0]
     emb = jnp.broadcast_to(emb[:, None], (2 * NOISE_FREQ, 128))
     nq, cw, rw, fl = nm // 2, D // nm, D // ne, 4 * D // nm
+    ny, nz = nm // 4, ne // 2
     own = 2 * REACH
     vm = pl.BlockSpec(memory_space=pltpu.VMEM)
     V = pltpu.VMEM
@@ -437,16 +487,18 @@
         V((2, 32, 128), F32), V((2, 32, 128), F32),
         V((LAYERS, own, 128), F32), V((LAYERS, 2, 8, 128), F32), V((LAYERS, 2, 8, 128), F32),
         V((own, D), BF16), V((own, D), BF16), V((own, D), BF16),
-        V((8, 2, nq, cw, D), BF16), V((8, nq, cw, D), BF16),
-        V((8, nq, cw, D), BF16), V((8, nq, cw, D), BF16),
-        V((2, 4 * cw, D), F32), V((2, ne, rw, 4 * cw), BF16), V((2, ne, rw, 4 * cw), BF16),
-        V((nq, 8, fl), F32), V((nq, 8, fl), F32), V((nq, 8, fl), F32), V((nq, 8, fl), F32),
-        V((8, fl), F32), V((ne, 8, fl), F32),
+        V((8, 2, 4 * ny, cw, 256), BF16), V((8, 4 * ny, cw, 256), BF16),
+        V((8, 4 * ny, cw, 256), BF16), V((8, 4, 4, cw, 256), BF16),
+        V((8, 4, cw, 256), BF16), V((8, 4, cw, 256), BF16),
+        V((2, 4 * cw, 256), F32), V((2, nz, rw, 4 * cw), BF16), V((2, nz, rw, 4 * cw), BF16),
+        V((nq, 8, fl), F32), V((nq, 8, fl), F32), V((nq, 8, fl), F32), V((ny, 2, 8, fl), F32),
+        V((2, 8, fl), F32), V((4, 8, fl), F32), V((2, 8, fl), F32), V((nz, 2, 8, fl), F32),
         pltpu.SemaphoreType.DMA((LAYERS, 4)),
         pltpu.SemaphoreType.DMA((7, 2)), pltpu.SemaphoreType.DMA((7, 2)),
         pltpu.SemaphoreType.DMA((9,)), pltpu.SemaphoreType.DMA((9,)),
-        pltpu.SemaphoreType.DMA((9, nq)), pltpu.SemaphoreType.DMA((9, nq)),
-        pltpu.SemaphoreType.DMA((3, ne)), pltpu.SemaphoreType.DMA((3, ne)),
+        pltpu.SemaphoreType.DMA((8, 4)), pltpu.SemaphoreType.DMA((8, 4)),
+        pltpu.SemaphoreType.DMA((8, 4)), pltpu.SemaphoreType.DMA((8, 4)),
+        pltpu.SemaphoreType.DMA((5, 8)), pltpu.SemaphoreType.DMA((5, 8)),
     ]
     outs = pl.pallas_call(
         functools.partial(kernel, ne, nm),

time: 80 us -> 74.5 us (0.931)
  Pallas kernels: 77.1 us -> 71.6 us
    pallas_call x1, Pallas kernels: 75.3 us -> 69.9 us  [body(): pl.pallas_call(functools.partial(kernel, ne, nm), out_shape=(jax.ShapeDty...]
where the time goes in v3:
time: 74.5 us; the launch traced here: 73.8 us
  Pallas kernels  71.6 us (96%)
  between operations  1.33 us (2%)
    pallas_call x1, Pallas kernels, body(): pl.pallas_call(functools.partial(kernel, ne, nm), out_shape=(jax.ShapeDty...  69.9 us
    pallas_call x1, Pallas kernels, body(): pl.pallas_call(hand_over, out_shape=tuple((jax.ShapeDtypeStruct(o.shape,...  1.78 us

profile of v3, /device:TPU:8, one launch (start us, length us, event | category | flops | bytes accessed | tf_op | source)
XLA Modules:
  0.0 73.8 jit_solution(7083195671686195206)
XLA Ops:
  1.4 0.1 maximum_bitcast_fusion
  1.4 0.7 broadcast_in_dim.10.emb_ref
  2.1 69.9 %shard_map.94 = (bf16[1,256,512]{2,1,0:T(8,128)(2,1)}, f32[2,4,32,32]{3,2,1,0:T(8,128)}, f32[2,32,64]{2,1,0:T(8,128)}) custom-call(bf16[1,256,512]{2,1,0:T(8,128)(2,1)} %x_ref.1, bf16[1,256,512]{2,1,0:T(8,128)(2,1)} %cot_ref.1, f32[32,128]{1,0:T(8,128)} %broadcast_in_dim.10.emb_ref, s32[32,256]{1,0:T(8,128)} %bitcast.5, s32[32,256]{1,0:T(8,128)} %bitcast.6, ...), custom_call_target="tpu_custom_call" | custom-call | tf_op jit(solution)/shard_map/pallas_call | solution.py:503
  72.0 1.8 %shard_map.95 = (bf16[1,256,512]{2,1,0:T(8,128)(2,1)}, f32[2,4,32,32]{3,2,1,0:T(8,128)}, f32[2,32,64]{2,1,0:T(8,128)}) custom-call(bf16[1,256,512]{2,1,0:T(8,128)(2,1)} %get-tuple-element.6.a_ref, f32[2,4,32,32]{3,2,1,0:T(8,128)} %get-tuple-element.7.b_ref, f32[2,32,64]{2,1,0:T(8,128)} %get-tuple-element.8.c_ref), custom_call_target="tpu_custom_call" | custom-call | tf_op jit(solution)/shard_map/pallas_call | solution.py:517
  (1 shorter events, 0.0 us)

commit v4 on v3

--- a/solution.py
+++ b/solution.py
@@ -17,6 +17,7 @@
 BF16 = jnp.bfloat16
 REACH = 128
 WIN = 3 * REACH
+CHUNK = 32
 D = 512
 HEAD = D // HEADS
 SCALE = 1.0 / math.sqrt(HEAD)
@@ -43,7 +44,7 @@
     gin_ref, gw_ref, gf_ref,
     w_v, hx1, hx2, hcot, hup, x2, up1, normed, unit, inv, qe, ke, ve, gae, prob, att,
     bias, bias_t, nl_own, nl_halo, stat, stat_own, stat_halo,
-    dq, dk, dv, wb, rc, s2, r2, t2, rt, acc, s3, r3, cond, rcond, s2f, ryf, sxf, rxf, s3f, r3f,
+    dq, dk, dv, raw_a, raw_b, half_a, half_b, normed_halo, gn_rows, wb, rc, s2, r2, t2, rt, acc, s3, r3, cond, rcond, s2f, ryf, sxf, rxf, s3f, r3f,
     w_sem, hs_sem, hr_sem, cs_sem, cr_sem, s2_sem, r2_sem, t2_sem, rt_sem, s3_sem, r3_sem,
 ):
     nq = nm // 2
@@ -146,38 +147,56 @@
         ve[layer, rows] = nn(n, w[2]).astype(BF16)
 
     def own_rows(src, layer):
-        def step(i, carry):
-            rows = pl.ds(pl.multiple_of(i * 64, 64), 64)
+        for i in range(2 * REACH // CHUNK):
+            rows = pl.ds(i * CHUNK, CHUNK)
             u, inverse, n = normalize(src[rows], layer)
             unit[layer, rows] = u
-            inv[layer, rows] = jnp.broadcast_to(inverse, (64, 128))
+            inv[layer, rows] = jnp.broadcast_to(inverse, (CHUNK, 128))
             normed[layer, rows] = n
-            return carry
-
-        lax.fori_loop(0, 4, step, 0)
         project_rows(pl.ds(REACH, 2 * REACH), normed[layer], layer)
 
     def halo_rows(src, layer):
         for side in range(2):
-            _, _, n = normalize(src[side], layer)
-            project_rows(pl.ds(side * 3 * REACH, REACH), n, layer)
+            for i in range(REACH // CHUNK):
+                rows = pl.ds(i * CHUNK, CHUNK)
+                _, _, n = normalize(src[side, rows], layer)
+                normed_halo[side, rows] = n
+            project_rows(pl.ds(side * 3 * REACH, REACH), normed_halo[side], layer)
+
+    BLOCKS = [(b, h) for b in range(2) for h in range(HEADS)]
+
+    def spans(b, h):
+        return (
+            pl.ds(REACH + b * REACH, REACH),
+            pl.ds(b * REACH, WIN),
+            slice(h * HEAD, (h + 1) * HEAD),
+            slice(b * REACH, (b + 1) * REACH),
+        )
+
+    def by_rows(step):
+        for b, h in BLOCKS:
+            for i in range(REACH // CHUNK):
+                step(b, h, pl.ds(i * CHUNK, CHUNK))
 
     def attend(layer):
-        for b in range(2):
-            rows = pl.ds(REACH + b * REACH, REACH)
-            window = pl.ds(b * REACH, WIN)
-            for h in range(HEADS):
-                cols = slice(h * HEAD, (h + 1) * HEAD)
-                s = nt(qe[layer, rows, cols], ke[layer, window, cols]) * SCALE2 + bias[b]
-                peak = jnp.max(s, axis=1, keepdims=True)
-                wts = jnp.exp2(s - peak)
-                total = jnp.sum(wts, axis=1, keepdims=True)
-                p = wts * (1.0 / total)
-                prob[layer, b * HEADS + h] = p
-                stat[layer, b * REACH:(b + 1) * REACH, h:h + 1] = peak + jnp.log2(total)
-                att[layer, b * REACH:(b + 1) * REACH, cols] = nn(
-                    p.astype(BF16), ve[layer, window, cols]
-                ).astype(BF16)
+        for b, h in BLOCKS:
+            rows, window, cols, _ = spans(b, h)
+            raw_a[b * HEADS + h] = nt(qe[layer, rows, cols], ke[layer, window, cols])
+
+        def soften(b, h, rows):
+            s = raw_a[b * HEADS + h, rows] * SCALE2 + bias[b, rows]
+            peak = jnp.max(s, axis=1, keepdims=True)
+            wts = jnp.exp2(s - peak)
+            total = jnp.sum(wts, axis=1, keepdims=True)
+            p = wts * (1.0 / total)
+            prob[layer, b * HEADS + h, rows] = p
+            half_a[b * HEADS + h, rows] = p.astype(BF16)
+            stat[layer, pl.ds(b * REACH + rows.start, CHUNK), h:h + 1] = peak + jnp.log2(total)
+
+        by_rows(soften)
+        for b, h in BLOCKS:
+            _, window, cols, own = spans(b, h)
+            att[layer, own, cols] = nn(half_a[b * HEADS + h], ve[layer, window, cols]).astype(BF16)
 
     def mask_tile(table, first):
         jid = (lax.broadcasted_iota(jnp.int32, (REACH, REACH), 0) + first).astype(F32)
@@ -233,40 +252,47 @@
     attend(1)
 
     def query_pass(layer):
-        for b in range(2):
-            rows = pl.ds(REACH + b * REACH, REACH)
-            window = pl.ds(b * REACH, WIN)
-            for h in range(HEADS):
-                cols = slice(h * HEAD, (h + 1) * HEAD)
-                gp = nt(gae[rows, cols], ve[layer, window, cols])
-                p = prob[layer, b * HEADS + h]
-                delta = jnp.sum(p * gp, axis=1, keepdims=True)
-                stat[layer, b * REACH:(b + 1) * REACH, HEADS + h:HEADS + h + 1] = delta
-                gs = (p * ((gp - delta) * SCALE)).astype(BF16)
-                dq[b * REACH:(b + 1) * REACH, cols] = nn(gs, ke[layer, window, cols]).astype(BF16)
+        for b, h in BLOCKS:
+            rows, window, cols, _ = spans(b, h)
+            raw_a[b * HEADS + h] = nt(gae[rows, cols], ve[layer, window, cols])
+
+        def differ(b, h, rows):
+            gp = raw_a[b * HEADS + h, rows]
+            p = prob[layer, b * HEADS + h, rows]
+            delta = jnp.sum(p * gp, axis=1, keepdims=True)
+            stat[layer, pl.ds(b * REACH + rows.start, CHUNK), HEADS + h:HEADS + h + 1] = delta
+            half_a[b * HEADS + h, rows] = (p * ((gp - delta) * SCALE)).astype(BF16)
+
+        by_rows(differ)
+        for b, h in BLOCKS:
+            _, window, cols, own = spans(b, h)
+            dq[own, cols] = nn(half_a[b * HEADS + h], ke[layer, window, cols]).astype(BF16)
         for half in range(2):
             stat_own[layer, half] = stat[layer, half * REACH:(half + 1) * REACH, :].T[0:8]
         return halo(5 + layer, stat_own.at[layer, 0], stat_own.at[layer, 1], stat_halo.at[layer])
 
     def key_pass(layer):
-        for jb in range(2):
-            rows = pl.ds(REACH + jb * REACH, REACH)
-            window = pl.ds(jb * REACH, WIN)
-            if jb == 0:
-                parts = [stat_halo[layer, 0], stat_own[layer, 0], stat_own[layer, 1]]
-            else:
-                parts = [stat_own[layer, 0], stat_own[layer, 1], stat_halo[layer, 1]]
-            stats = jnp.concatenate(parts, axis=1)
-            for h in range(HEADS):
-                cols = slice(h * HEAD, (h + 1) * HEAD)
-                queries = qe[layer, window, cols]
-                grads = gae[window, cols]
-                s = nt(ke[layer, rows, cols], queries) * SCALE2 + bias_t[jb]
-                p = jnp.exp2(s - stats[h:h + 1])
-                gp = nt(ve[layer, rows, cols], grads)
-                gs = (p * ((gp - stats[HEADS + h:HEADS + h + 1]) * SCALE)).astype(BF16)
-                dk[jb * REACH:(jb + 1) * REACH, cols] = nn(gs, queries).astype(BF16)
-                dv[jb * REACH:(jb + 1) * REACH, cols] = nn(p.astype(BF16), grads).astype(BF16)
+        for jb, h in BLOCKS:
+            rows, window, cols, _ = spans(jb, h)
+            raw_a[jb * HEADS + h] = nt(ke[layer, rows, cols], qe[layer, window, cols])
+            raw_b[jb * HEADS + h] = nt(ve[layer, rows, cols], gae[window, cols])
+        stats = (
+            jnp.concatenate([stat_halo[layer, 0], stat_own[layer, 0], stat_own[layer, 1]], axis=1),
+            jnp.concatenate([stat_own[layer, 0], stat_own[layer, 1], stat_halo[layer, 1]], axis=1),
+        )
+
+        def differ(jb, h, rows):
+            s = raw_a[jb * HEADS + h, rows] * SCALE2 + bias_t[jb, rows]
+            p = jnp.exp2(s - stats[jb][h:h + 1])
+            gp = raw_b[jb * HEADS + h, rows]
+            half_a[jb * HEADS + h, rows] = (p * ((gp - stats[jb][HEADS + h:HEADS + h + 1]) * SCALE)).astype(BF16)
+            half_b[jb * HEADS + h, rows] = p.astype(BF16)
+
+        by_rows(differ)
+        for jb, h in BLOCKS:
+            _, window, cols, own = spans(jb, h)
+            dk[own, cols] = nn(half_a[jb * HEADS + h], qe[layer, window, cols]).astype(BF16)
+            dv[own, cols] = nn(half_b[jb * HEADS + h], gae[window, cols]).astype(BF16)
 
     def order(batch):
         return ((ny, y, at_y), (4, x, at_x)) if batch % 2 == 0 else ((4, x, at_x), (ny, y, at_y))
@@ -341,16 +367,21 @@
 
     def input_rows(layer, up, out, i):
         w = w_v.at[layer]
-        rows = pl.ds(i * REACH, REACH)
-        gn = nt(dq[rows], w[0]) + nt(dk[rows], w[1]) + nt(dv[rows], w[2])
-        u = unit[layer, rows]
-        gu = gn * u
-        first = jnp.sum(gu, axis=0, keepdims=True)
-        second = jnp.sum(gn, axis=0, keepdims=True)
-        mean_g = jnp.mean(gn * scales[layer], axis=1, keepdims=True)
-        mean_gu = jnp.mean(gu * scales[layer], axis=1, keepdims=True)
-        centred = gn * scales[layer] - mean_g - u * mean_gu
-        out[rows] = (up[rows].astype(F32) + inv[layer, rows][:, 0:1] * centred).astype(BF16)
+        block = pl.ds(i * REACH, REACH)
+        gn_rows[...] = nt(dq[block], w[0]) + nt(dk[block], w[1]) + nt(dv[block], w[2])
+        first, second = jnp.zeros((1, D), F32), jnp.zeros((1, D), F32)
+        for j in range(REACH // CHUNK):
+            rows = pl.ds(i * REACH + j * CHUNK, CHUNK)
+            gn = gn_rows[pl.ds(j * CHUNK, CHUNK)]
+            u = unit[layer, rows]
+            gu = gn * u
+            first = first + jnp.sum(gu, axis=0, keepdims=True)
+            second = second + jnp.sum(gn, axis=0, keepdims=True)
+            g = gn * scales[layer]
+            mean_g = jnp.mean(g, axis=1, keepdims=True)
+            mean_gu = jnp.mean(gu * scales[layer], axis=1, keepdims=True)
+            centred = g - mean_g - u * mean_gu
+            out[rows] = (up[rows].astype(F32) + inv[layer, rows][:, 0:1] * centred).astype(BF16)
         return jnp.concatenate([first, second], axis=1)
 
     def put_cond(layer, row):
@@ -386,12 +417,12 @@
     ring_of[4] = core_sum(4, core_of[4])
     wait_recv((up_a, up_b))
     grad_attended(up1, hup, 0, 1)
+    ring_of[5] = core_sum(5, core_of[5])
+    turn_of[1] = first_sum(1, ring_of[1])
     wait_recv(st)
     key_pass(0)
     core_of[6] = weight_grad(6, dk, normed.at[0])
     core_of[7] = weight_grad(7, dv, normed.at[0])
-    ring_of[5] = core_sum(5, core_of[5])
-    turn_of[1] = first_sum(1, ring_of[1])
     row = input_rows(0, up1, gin_ref.at[0], 0)
     ring_of[6] = core_sum(6, core_of[6])
     ring_of[7] = core_sum(7, core_of[7])
@@ -487,6 +518,9 @@
         V((2, 32, 128), F32), V((2, 32, 128), F32),
         V((LAYERS, own, 128), F32), V((LAYERS, 2, 8, 128), F32), V((LAYERS, 2, 8, 128), F32),
         V((own, D), BF16), V((own, D), BF16), V((own, D), BF16),
+        V((2 * HEADS, REACH, WIN), F32), V((2 * HEADS, REACH, WIN), F32),
+        V((2 * HEADS, REACH, WIN), BF16), V((2 * HEADS, REACH, WIN), BF16),
+        V((2, REACH, D), BF16), V((REACH, D), F32),
         V((8, 2, 4 * ny, cw, 256), BF16), V((8, 4 * ny, cw, 256), BF16),
         V((8, 4 * ny, cw, 256), BF16), V((8, 4, 4, cw, 256), BF16),
         V((8, 4, cw, 256), BF16), V((8, 4, cw, 256), BF16),

time: 74.5 us -> 67.6 us (0.907)
  Pallas kernels: 71.6 us -> 65.3 us
    pallas_call x1, Pallas kernels: 69.9 us -> 63.5 us  [body(): pl.pallas_call(functools.partial(kernel, ne, nm), out_shape=(jax.ShapeDty...]
where the time goes in v4:
time: 67.6 us; the launch traced here: 67.4 us
  Pallas kernels  65.3 us (97%)
  between operations  1.33 us (2%)
  local copies, waits for them, and re-layouts  0.68 us (1%)
    pallas_call x1, Pallas kernels, body(): pl.pallas_call(functools.partial(kernel, ne, nm), out_shape=(jax.ShapeDty...  63.5 us
    pallas_call x1, Pallas kernels, body(): pl.pallas_call(hand_over, out_shape=tuple((jax.ShapeDtypeStruct(o.shape,...  1.78 us

profile of v4, /device:TPU:8, one launch (start us, length us, event | category | flops | bytes accessed | tf_op | source)
XLA Modules:
  0.0 67.4 jit_solution(11022251752929231004)
XLA Ops:
  1.4 0.1 maximum_bitcast_fusion
  1.4 0.7 %broadcast_in_dim.10.emb_ref = f32[32,128]{1,0:T(8,128)} broadcast(f32[32]{0:T(128)S(1)} %maximum_bitcast_fusion), dimensions={0} | broadcast | bytes 16512 | tf_op jit(solution)/shard_map/broadcast_in_dim | solution.py:503
  2.1 63.5 %shard_map.94 = (bf16[1,256,512]{2,1,0:T(8,128)(2,1)}, f32[2,4,32,32]{3,2,1,0:T(8,128)}, f32[2,32,64]{2,1,0:T(8,128)}) custom-call(bf16[1,256,512]{2,1,0:T(8,128)(2,1)} %x_ref.1, bf16[1,256,512]{2,1,0:T(8,128)(2,1)} %cot_ref.1, f32[32,128]{1,0:T(8,128)} %broadcast_in_dim.10.emb_ref, s32[32,256]{1,0:T(8,128)} %bitcast.5, s32[32,256]{1,0:T(8,128)} %bitcast.6, ...), custom_call_target="tpu_custom_call" | custom-call | tf_op jit(solution)/shard_map/pallas_call | solution.py:537
  65.6 1.8 %shard_map.95 = (bf16[1,256,512]{2,1,0:T(8,128)(2,1)}, f32[2,4,32,32]{3,2,1,0:T(8,128)}, f32[2,32,64]{2,1,0:T(8,128)}) custom-call(bf16[1,256,512]{2,1,0:T(8,128)(2,1)} %get-tuple-element.6.a_ref, f32[2,4,32,32]{3,2,1,0:T(8,128)} %get-tuple-element.7.b_ref, f32[2,32,64]{2,1,0:T(8,128)} %get-tuple-element.8.c_ref), custom_call_target="tpu_custom_call" | custom-call | tf_op jit(solution)/shard_map/pallas_call | solution.py:551
  (1 shorter events, 0.0 us)

commit v5 on v4

--- a/solution.py
+++ b/solution.py
@@ -393,9 +393,10 @@
     core_of[0] = weight_grad(0, cot_ref.at[0], att.at[1])
     st = query_pass(1)
     sent.extend(st)
+    ring_of[0] = core_sum(0, core_of[0])
     core_of[1] = weight_grad(1, dq, normed.at[1])
-    ring_of[0] = core_sum(0, core_of[0])
     wait_recv(st)
+    ring_of[1] = core_sum(1, core_of[1])
     key_pass(1)
     row = input_rows(1, cot_ref.at[0], up1, 0)
     up_a = rcopy(up1.at[LOW], hup.at[1], hs_sem.at[4, 1], hr_sem.at[4, 1], e, left)
@@ -404,7 +405,6 @@
     put_cond(1, row)
     core_of[2] = weight_grad(2, dk, normed.at[1])
     core_of[3] = weight_grad(3, dv, normed.at[1])
-    ring_of[1] = core_sum(1, core_of[1])
     core_of[4] = weight_grad(4, up1, att.at[0])
     grad_attended(up1[...], hup, 0, 0)
 

time: 67.6 us -> 66.4 us (0.982)
  Pallas kernels: 65.3 us -> 63.6 us
    pallas_call x1, Pallas kernels: 63.5 us -> 61.8 us  [body(): pl.pallas_call(functools.partial(kernel, ne, nm), out_shape=(jax.ShapeDty...]
where the time goes in v5:
time: 66.4 us; the launch traced here: 65.7 us
  Pallas kernels  63.6 us (96%)
  between operations  1.33 us (2%)
  local copies, waits for them, and re-layouts  0.68 us (1%)
    pallas_call x1, Pallas kernels, body(): pl.pallas_call(functools.partial(kernel, ne, nm), out_shape=(jax.ShapeDty...  61.8 us
    pallas_call x1, Pallas kernels, body(): pl.pallas_call(hand_over, out_shape=tuple((jax.ShapeDtypeStruct(o.shape,...  1.78 us

profile of v5, /device:TPU:8, one launch (start us, length us, event | category | flops | bytes accessed | tf_op | source)
XLA Modules:
  0.0 65.7 jit_solution(4446971350855601463)
XLA Ops:
  1.4 0.1 maximum_bitcast_fusion
  1.4 0.7 %broadcast_in_dim.10.emb_ref = f32[32,128]{1,0:T(8,128)} broadcast(f32[32]{0:T(128)S(1)} %maximum_bitcast_fusion), dimensions={0} | broadcast | bytes 16512 | tf_op jit(solution)/shard_map/broadcast_in_dim | solution.py:503
  2.1 61.8 %shard_map.94 = (bf16[1,256,512]{2,1,0:T(8,128)(2,1)}, f32[2,4,32,32]{3,2,1,0:T(8,128)}, f32[2,32,64]{2,1,0:T(8,128)}) custom-call(bf16[1,256,512]{2,1,0:T(8,128)(2,1)} %x_ref.1, bf16[1,256,512]{2,1,0:T(8,128)(2,1)} %cot_ref.1, f32[32,128]{1,0:T(8,128)} %broadcast_in_dim.10.emb_ref, s32[32,256]{1,0:T(8,128)} %bitcast.5, s32[32,256]{1,0:T(8,128)} %bitcast.6, ...), custom_call_target="tpu_custom_call" | custom-call | tf_op jit(solution)/shard_map/pallas_call | solution.py:537
  63.9 1.8 %shard_map.95 = (bf16[1,256,512]{2,1,0:T(8,128)(2,1)}, f32[2,4,32,32]{3,2,1,0:T(8,128)}, f32[2,32,64]{2,1,0:T(8,128)}) custom-call(bf16[1,256,512]{2,1,0:T(8,128)(2,1)} %get-tuple-element.6.a_ref, f32[2,4,32,32]{3,2,1,0:T(8,128)} %get-tuple-element.7.b_ref, f32[2,32,64]{2,1,0:T(8,128)} %get-tuple-element.8.c_ref), custom_call_target="tpu_custom_call" | custom-call | tf_op jit(solution)/shard_map/pallas_call | solution.py:551
  (1 shorter events, 0.0 us)
